TPU v7x, 32 devices: a whole 2x2x4 slice. The times are simulated.
32 devices in a mesh: grp: 2 (over x), pix: 8 (over z, y), disp: 2 (over core).
Axes of the slice: x: 2, y: 2, z: 4, core: 2. Of those that a mesh axis runs over, the one named last changes fastest.
Arguments:
- left_image: int32 [128, 1024], P(('grp', 'pix')), parts along dimension 0, may hold values from 0 to 255
- right_image: int32 [128, 1024], P(('grp', 'pix')), parts along dimension 0, may hold values from 0 to 255
- feat_weight: float32 [16, 16], replicated, may hold values from -1.5 to 1.5
- first_weight: bfloat16 [3, 3, 3, 16, 16], replicated, may hold values from -0.3125 to 0.3125
- first_bias: float32 [16], replicated, may hold values from -3 to 3
- second_weight: bfloat16 [3, 3, 3, 16, 16], replicated, may hold values from -0.3125 to 0.3125
- second_bias: float32 [16], replicated, may hold values from -3 to 3
- head_weight: float32 [16], replicated, may hold values from -1.5 to 1.5
- mask_weight: float32 [16, 144], replicated, may hold values from -1.5 to 1.5
- confidence: float32 [128, 1024], P(('grp', 'pix')), parts along dimension 0, may hold values from 0.1 to 1
Outputs:
- coarse_disparity: float32 [32, 256], P(('grp', 'pix')), parts along dimension 0
- disparity_map: float32 [128, 1024], P(('grp', 'pix')), parts along dimension 0
There are 2 independent parts, one for each index of `grp`. A program takes and returns all parts, laid end to end along the dimension named above; an argument that names none is the same for every part. Nothing has to cross between parts.
All inputs are finite; a program needn't handle non-finite values.
Results may differ from a plain program's by a relative error of at most 0.0065.
Values may be sent and summed in bfloat16 or wider, within the bound.
A program may use at most 64 MiB of HBM per device.

v0:
```python
import jax
import jax.numpy as jnp
from jax import lax
from jax.sharding import PartitionSpec as P

DSP = 128
UP = 4
TV_ITERS = 8


dual_step = 0.175
primal_step = 0.7
tv_bound = 0.3
cost_scale = 8.0
mask_scale = 3.0
highest_prec = lax.Precision.HIGHEST


def with_halo(value, sides, width):
    for axis, dim in sides:
        size, length = (lax.axis_size(axis), value.shape[dim])
        up = [(i, (i + 1) % size) for i in range(size - 1)]
        down = [(j, i) for i, j in up]
        last = lax.slice_in_dim(value, length - width, length, axis=dim)
        leading = lax.slice_in_dim(value, 0, width, axis=dim)
        before = lax.ppermute(last, axis, up)
        after = lax.ppermute(leading, axis, down)
        value = jnp.concatenate([before, value, after], axis=dim)
    return value


def features(image, feat_weight):
    pixels = image.astype(jnp.float32) / 64.0 - 2.0
    row_count = image.shape[0] // UP
    col_count = image.shape[1] // UP
    patches = (
        pixels.reshape(row_count, UP, col_count, UP)
        .transpose(1, 3, 0, 2)
        .reshape(UP * UP, row_count, col_count)
    )
    return jnp.einsum("pc,prw->crw", feat_weight, patches, precision=highest_prec).astype(
        jnp.bfloat16
    )


def cost_volume(left_feat, right_feat, planes):
    col_count = right_feat.shape[2]
    padded = jnp.pad(right_feat, ((0, 0), (0, 0), (DSP, 0)))

    def take_plane(plane):
        return lax.dynamic_slice_in_dim(padded, DSP - plane, col_count, 2)

    shifted = jax.vmap(take_plane)(planes)
    return (left_feat.astype(jnp.float32)[None] * shifted.astype(jnp.float32)).astype(jnp.bfloat16)


def conv_valid(padded, weights):
    plane_total = padded.shape[0] - 2
    channels = padded.shape[1]
    row_count = padded.shape[2] - 2
    col_count = padded.shape[3]
    widened = jnp.pad(padded, ((0, 0), (0, 0), (0, 0), (1, 1)))
    columns = jnp.concatenate(
        [
            widened[:, :, shift_y : shift_y + row_count, shift_x : shift_x + col_count]
            for shift_y in range(3)
            for shift_x in range(3)
        ],
        axis=1,
    )
    folded = weights.reshape(3, 9 * channels, weights.shape[4])
    summed = jnp.einsum(
        "dkrw,ko->dorw", columns[0:plane_total], folded[0], preferred_element_type=jnp.float32
    )
    for shift_d in range(1, 3):
        summed = summed + jnp.einsum(
            "dkrw,ko->dorw",
            columns[shift_d : shift_d + plane_total],
            folded[shift_d],
            preferred_element_type=jnp.float32,
        )
    return summed


def upsample(rimmed, left_feat, mask_weight):
    row_count = rimmed.shape[0] - 2
    col_count = rimmed.shape[1]
    logits = mask_scale * jnp.tanh(
        jnp.einsum(
            "ck,crw->krw", mask_weight, left_feat.astype(jnp.float32), precision=highest_prec
        )
    )
    expo = jnp.exp(logits).reshape(9, UP * UP, row_count, col_count)
    mixing = expo / jnp.sum(expo, 0)
    widened = jnp.pad(rimmed, ((0, 0), (1, 1)))
    neighbours = jnp.stack(
        [
            widened[shift_y : shift_y + row_count, shift_x : shift_x + col_count]
            for shift_y in range(3)
            for shift_x in range(3)
        ]
    )
    subpixel = jnp.sum(mixing * neighbours[:, None], 0)
    return (
        subpixel.reshape(UP, UP, row_count, col_count)
        .transpose(2, 0, 3, 1)
        .reshape(row_count * UP, col_count * UP)
    )


def zero_row(values):
    return jnp.zeros_like(values[:1])


def tv_iter(current, target, fidelity, global_fine, row_total, fetch_below, fetch_above):
    primal, extrap, dual_x, dual_y = current
    below_row = fetch_below(extrap)
    downward = jnp.concatenate([extrap[1:], below_row], 0)
    inside = ((global_fine >= 0) & (global_fine < row_total - 1))[:, None]
    grad_y = jnp.where(inside, downward - extrap, 0.0)
    grad_x = jnp.concatenate([extrap[:, 1:] - extrap[:, :-1], jnp.zeros_like(extrap[:, :1])], 1)
    trial_x = dual_x + dual_step * grad_x
    trial_y = dual_y + dual_step * grad_y
    shrink = jnp.maximum(1.0, jnp.sqrt(trial_x * trial_x + trial_y * trial_y) / tv_bound)
    dual_x = trial_x / shrink
    dual_y = trial_y / shrink
    above_row = fetch_above(dual_y)
    upper = jnp.concatenate([above_row, dual_y[:-1]], 0)
    left_col = jnp.concatenate([jnp.zeros_like(dual_x[:, :1]), dual_x[:, :-1]], 1)
    divergence = dual_x - left_col + dual_y - upper
    updated = (primal + primal_step * divergence + primal_step * fidelity * target) / (
        1.0 + primal_step * fidelity
    )
    return (updated, 2.0 * updated - primal, dual_x, dual_y)


def local(
    left_image,
    right_image,
    feat_weight,
    first_weight,
    first_bias,
    second_weight,
    second_bias,
    head_weight,
    mask_weight,
    confidence,
):
    left_feat = features(left_image, feat_weight)
    right_feat = features(right_image, feat_weight)
    plane_count = DSP // lax.axis_size("disp")
    plane_start = lax.axis_index("disp") * plane_count
    planes = plane_start + jnp.arange(plane_count, dtype=jnp.int32)
    first_shift = first_bias[None, :, None, None]
    volume = cost_volume(left_feat, right_feat, planes)
    padded = with_halo(volume, (("pix", 2), ("disp", 0)), 1)
    hidden = jax.nn.relu(conv_valid(padded, first_weight) + first_shift).astype(jnp.bfloat16)
    padded = with_halo(hidden, (("pix", 2), ("disp", 0)), 1)
    second = jax.nn.relu(conv_valid(padded, second_weight) + second_bias[None, :, None, None])
    raw_score = jnp.einsum("dorw,o->drw", second, head_weight, precision=highest_prec)
    match_cost = cost_scale * jnp.tanh(raw_score)
    expo = jnp.exp(-match_cost)
    plane_frac = planes.astype(jnp.float32) / DSP
    total_weight, total_plane = lax.psum(
        (jnp.sum(expo, 0), jnp.sum(expo * plane_frac[:, None, None], 0)), "disp"
    )
    coarse = total_plane / total_weight
    rimmed = with_halo(coarse, (("pix", 0),), 1)
    initial = upsample(rimmed, left_feat, mask_weight)
    fine_rows = initial.shape[0]
    row_total = fine_rows * lax.axis_size("pix")
    stacked = jnp.stack([initial, confidence])
    extended_fine = with_halo(stacked.astype(jnp.bfloat16), (("pix", 1),), TV_ITERS).astype(
        stacked.dtype
    )
    target = extended_fine[0]
    fidelity = extended_fine[1]
    global_fine = (
        lax.axis_index("pix") * fine_rows
        - TV_ITERS
        + jnp.arange(fine_rows + 2 * TV_ITERS, dtype=jnp.int32)
    )
    margin = TV_ITERS
    current = (target, target, jnp.zeros_like(target), jnp.zeros_like(target))
    for step_index in range(TV_ITERS):
        current = tv_iter(current, target, fidelity, global_fine, row_total, zero_row, zero_row)
    result = current[0][margin : margin + fine_rows]
    return (coarse, result)


def solution(mesh):
    placed = (
        P(("grp", "pix"), None),
        P(("grp", "pix"), None),
        P(),
        P(),
        P(),
        P(),
        P(),
        P(),
        P(),
        P(("grp", "pix"), None),
    )
    return jax.shard_map(
        local,
        mesh=mesh,
        in_specs=placed,
        out_specs=(P(("grp", "pix"), None), P(("grp", "pix"), None)),
        check_vma=False,
    )
```

profile of v0, /device:TPU:0, one launch (start us, length us, event | category | flops | bytes accessed | tf_op | source)
XLA Modules:
  0.0 152.5 jit_solution(6051076933376511878)
XLA Ops:
  4.1 19.3 %gather_fusion = bf16[64,16,2,256]{1,2,3,0:T(2,128)(2,1)} fusion(bf16[16,2,384]{0,1,2:T(2,128)(2,1)S(1)} %pad.48.clone, s32[64]{0:T(128)S(1)} %shift-left_bitcast_fusion), kind=kCustom, calls=%fused_computation | custom fusion | bytes 2097920 | tf_op jit(solution)/shard_map/vmap()/gather | solution.py:51
  23.3 15.6 %copy.87 = bf16[64,16,2,256]{3,1,2,0:T(8,128)(2,1)S(1)} copy(bf16[64,16,2,256]{1,2,3,0:T(2,128)(2,1)} %gather_fusion) | data formatting | bytes 2097152 | tf_op jit(solution)/shard_map/vmap()/gather | solution.py:51
  41.0 4.9 %collective-permute-start = (bf16[64,16,1,256]{3,1,2,0:T(8,128)(2,1)S(1)}, bf16[64,16,1,256]{3,1,2,0:T(8,128)(2,1)S(1)}, u32[]{:S(2)}, u32[]{:S(2)}) collective-permute-start(bf16[64,16,1,256]{3,1,2,0:T(8,128)(2,1)S(1)} %get-tuple-element.41), channel_id=1, source_target_pairs={{0,2},{2,4},{4,6},{6,8},{8,10},{10,12},{12,14},{1,3},{3,5},{5,7},{... | collective-permute-start | bytes 1572872 | tf_op jit(solution)/shard_map/ppermute | solution.py:26
  45.9 1.3 collective-permute-start.1
  47.2 21.1 %collective-permute-done = bf16[64,16,1,256]{3,1,2,0:T(8,128)(2,1)S(1)} collective-permute-done((bf16[64,16,1,256]{3,1,2,0:T(8,128)(2,1)S(1)}, bf16[64,16,1,256]{3,1,2,0:T(8,128)(2,1)S(1)}, u32[]{:S(2)}, u32[]{:S(2)}) %collective-permute-start) | collective-permute-done | bytes 524320 | tf_op jit(solution)/shard_map/ppermute | solution.py:26
  69.6 1.5 collective-permute-start.3
  71.1 1.6 %collective-permute-done.3 = bf16[1,16,4,256]{3,1,2,0:T(8,128)(2,1)S(1)} collective-permute-done((bf16[1,16,4,256]{3,1,2,0:T(8,128)(2,1)S(1)}, bf16[1,16,4,256]{3,1,2,0:T(8,128)(2,1)S(1)}, u32[]{:S(2)}, u32[]{:S(2)}) %collective-permute-start.3) | collective-permute-done | bytes 32800 | tf_op jit(solution)/shard_map/ppermute | solution.py:27
  76.2 1.4 fusion.8
  77.6 1.4 fusion.10
  79.0 1.4 fusion.20
  80.5 4.4 %collective-permute-start.4 = (bf16[64,16,1,256]{3,1,2,0:T(8,128)(2,1)S(1)}, bf16[64,16,1,256]{3,1,2,0:T(8,128)(2,1)S(1)}, u32[]{:S(2)}, u32[]{:S(2)}) collective-permute-start(bf16[64,16,1,256]{3,1,2,0:T(8,128)(2,1)S(1)} %get-tuple-element.39), channel_id=1, source_target_pairs={{0,2},{2,4},{4,6},{6,8},{8,10},{10,12},{12,14},{1,3},{3,5},{5,7},{... | collective-permute-start | bytes 1572872 | tf_op jit(solution)/shard_map/ppermute | solution.py:26
  84.9 1.3 collective-permute-start.5
  86.6 21.0 %collective-permute-done.4 = bf16[64,16,1,256]{3,1,2,0:T(8,128)(2,1)S(1)} collective-permute-done((bf16[64,16,1,256]{3,1,2,0:T(8,128)(2,1)S(1)}, bf16[64,16,1,256]{3,1,2,0:T(8,128)(2,1)S(1)}, u32[]{:S(2)}, u32[]{:S(2)}) %collective-permute-start.4) | collective-permute-done | bytes 524320 | tf_op jit(solution)/shard_map/ppermute | solution.py:26
  108.9 1.5 collective-permute-start.7
  110.4 1.6 %collective-permute-done.7 = bf16[1,16,4,256]{3,1,2,0:T(8,128)(2,1)S(1)} collective-permute-done((bf16[1,16,4,256]{3,1,2,0:T(8,128)(2,1)S(1)}, bf16[1,16,4,256]{3,1,2,0:T(8,128)(2,1)S(1)}, u32[]{:S(2)}, u32[]{:S(2)}) %collective-permute-start.7) | collective-permute-done | bytes 32800 | tf_op jit(solution)/shard_map/ppermute | solution.py:27
  115.5 1.4 fusion.2
  116.9 1.4 fusion.4
  118.3 1.4 fusion
  119.7 1.5 %fusion.12 = f32[1,64,2,256]{3,0,2,1:T(1,128)S(1)} fusion(f32[64,2,256,16]{2,3,1,0:T(8,128)S(1)} %fusion, f32[64,2,256,16]{2,3,1,0:T(8,128)S(1)} %fusion.4, f32[64,2,256,16]{2,3,1,0:T(8,128)S(1)} %fusion.2, f32[16]{0:T(128)S(1)} %copy-done.8, f32[16]{0:T(128)S(1)} %copy-done.9), kind=kOutput, calls=%fused_computation.27 | convolution fusion | flops 8388608 | bytes 6422656 | tf_op jit(solution)/shard_map/dorw,o->drw/dot_general | solution.py:160
  121.3 2.5 %all-reduce.37 = (f32[2,256]{1,0:T(2,128)S(1)}, f32[2,256]{1,0:T(2,128)S(1)}) all-reduce(f32[2,256]{1,0:T(2,128)S(1)} %get-tuple-element.3, f32[2,256]{1,0:T(2,128)S(1)} %get-tuple-element.2), channel_id=1, replica_groups=mesh['grp'=2,'pix'=8,'disp'=2] {'disp'}, use_global_device_ids=true, to_apply=%region_1.2 | all-reduce | flops 1024 | bytes 8192 | tf_op jit(solution)/shard_map/psum | solution.py:164
  123.8 4.4 %collective-permute-start.8 = (f32[1,256]{1,0:T(1,128)S(1)}, f32[1,256]{1,0:T(1,128)S(1)}, u32[]{:S(2)}, u32[]{:S(2)}) collective-permute-start(f32[1,256]{1,0:T(1,128)S(1)} %get-tuple-element.52), channel_id=1, source_target_pairs={{0,2},{2,4},{4,6},{6,8},{8,10},{10,12},{12,14},{1,3},{3,5},{5,7},{... | collective-permute-start | bytes 3080 | tf_op jit(solution)/shard_map/ppermute | solution.py:26
  129.6 6.7 %collective-permute-done.9 = f32[1,256]{1,0:T(1,128)S(1)} collective-permute-done((f32[1,256]{1,0:T(1,128)S(1)}, f32[1,256]{1,0:T(1,128)S(1)}, u32[]{:S(2)}, u32[]{:S(2)}) %collective-permute-start.9) | collective-permute-done | bytes 1056 | tf_op jit(solution)/shard_map/ppermute | solution.py:27
  137.9 4.8 %collective-permute-start.10 = (bf16[2,8,1024]{2,1,0:T(8,128)(2,1)S(1)}, bf16[2,8,1024]{2,1,0:T(8,128)(2,1)S(1)}, u32[]{:S(2)}, u32[]{:S(2)}) collective-permute-start(bf16[2,8,1024]{2,1,0:T(8,128)(2,1)S(1)} %pad_maximum_fusion.8), channel_id=1, source_target_pairs={{0,2},{2,4},{4,6},{6,8},{8,10},{10,12},{12,14},{1,3},{3,5},{5,7},{... | collective-permute-start | bytes 98312 | tf_op jit(solution)/shard_map/ppermute | solution.py:26
  144.3 4.2 %collective-permute-done.11 = bf16[2,8,1024]{2,1,0:T(8,128)(2,1)S(1)} collective-permute-done((bf16[2,8,1024]{2,1,0:T(8,128)(2,1)S(1)}, bf16[2,8,1024]{2,1,0:T(8,128)(2,1)S(1)}, u32[]{:S(2)}, u32[]{:S(2)}) %collective-permute-start.11) | collective-permute-done | bytes 32800 | tf_op jit(solution)/shard_map/ppermute | solution.py:27
  (133 shorter events, 23.8 us)
Async XLA Ops:
  0.6 85.6 %copy-start = (f32[16,144]{1,0:T(8,128)S(1)}, f32[16,144]{1,0:T(8,128)}, u32[]{:S(2)}) copy-start(f32[16,144]{1,0:T(8,128)} %param.18) | copy-start | bytes 27652
  23.3 15.6 %copy-start.5 = (s32[8,1024]{1,0:T(8,128)S(1)}, s32[8,1024]{1,0:T(8,128)}, u32[]{:S(2)}) copy-start(s32[8,1024]{1,0:T(8,128)} %param.10) | copy-start | bytes 98308
  23.3 17.0 %copy-start.6 = (f32[16,16]{1,0:T(8,128)S(1)}, f32[16,16]{1,0:T(8,128)}, u32[]{:S(2)}) copy-start(f32[16,16]{1,0:T(8,128)} %param.12) | copy-start | bytes 3076
  40.4 30.7 %copy-start.1 = (bf16[3,3,3,16,16]{4,3,2,1,0:T(8,128)(2,1)S(1)}, bf16[3,3,3,16,16]{4,3,2,1,0:T(8,128)(2,1)}, u32[]{:S(2)}) copy-start(bf16[3,3,3,16,16]{4,3,2,1,0:T(8,128)(2,1)} %param.13) | copy-start | bytes 41476
  41.0 27.3 %collective-permute-start = (bf16[64,16,1,256]{3,1,2,0:T(8,128)(2,1)S(1)}, bf16[64,16,1,256]{3,1,2,0:T(8,128)(2,1)S(1)}, u32[]{:S(2)}, u32[]{:S(2)}) collective-permute-start(bf16[64,16,1,256]{3,1,2,0:T(8,128)(2,1)S(1)} %get-tuple-element.41), channel_id=1, source_target_pairs={{0,2},{2,4},{4,6},{6,8},{8,10},{10,12},{12,14},{1,3},{3,5},{5,7},{... | collective-permute-start | bytes 1572872 | tf_op jit(solution)/shard_map/ppermute | solution.py:26
  45.9 22.4 %collective-permute-start.1 = (bf16[64,16,1,256]{3,1,2,0:T(8,128)(2,1)S(1)}, bf16[64,16,1,256]{3,1,2,0:T(8,128)(2,1)S(1)}, u32[]{:S(2)}, u32[]{:S(2)}) collective-permute-start(bf16[64,16,1,256]{3,1,2,0:T(8,128)(2,1)S(1)} %get-tuple-element.42), channel_id=1, source_target_pairs={{2,0},{4,2},{6,4},{8,6},{10,8},{12,10},{14,12},{3,1},{5,3},{7,5},{... | collective-permute-start | bytes 1572872 | tf_op jit(solution)/shard_map/ppermute | solution.py:27
  68.3 2.8 %collective-permute-start.2 = (bf16[1,16,4,256]{3,1,2,0:T(8,128)(2,1)S(1)}, bf16[1,16,4,256]{3,1,2,0:T(8,128)(2,1)S(1)}, u32[]{:S(2)}, u32[]{:S(2)}) collective-permute-start(bf16[1,16,4,256]{3,1,2,0:T(8,128)(2,1)S(1)} %get-tuple-element.37), channel_id=1, source_target_pairs={{0,1},{2,3},{4,5},{6,7},{8,9},{10,11},{12,13},{14,15},{16,17},{18,... | collective-permute-start | bytes 98312 | tf_op jit(solution)/shard_map/ppermute | solution.py:26
  69.6 3.1 %collective-permute-start.3 = (bf16[1,16,4,256]{3,1,2,0:T(8,128)(2,1)S(1)}, bf16[1,16,4,256]{3,1,2,0:T(8,128)(2,1)S(1)}, u32[]{:S(2)}, u32[]{:S(2)}) collective-permute-start(bf16[1,16,4,256]{3,1,2,0:T(8,128)(2,1)S(1)} %get-tuple-element.38), channel_id=1, source_target_pairs={{1,0},{3,2},{5,4},{7,6},{9,8},{11,10},{13,12},{15,14},{17,16},{19,... | collective-permute-start | bytes 98312 | tf_op jit(solution)/shard_map/ppermute | solution.py:27
  77.6 1.4 copy-start.7
  79.0 7.2 %copy-start.2 = (bf16[3,3,3,16,16]{4,3,2,1,0:T(8,128)(2,1)S(1)}, bf16[3,3,3,16,16]{4,3,2,1,0:T(8,128)(2,1)}, u32[]{:S(2)}) copy-start(bf16[3,3,3,16,16]{4,3,2,1,0:T(8,128)(2,1)} %param.15) | copy-start | bytes 41476
  80.5 27.1 %collective-permute-start.4 = (bf16[64,16,1,256]{3,1,2,0:T(8,128)(2,1)S(1)}, bf16[64,16,1,256]{3,1,2,0:T(8,128)(2,1)S(1)}, u32[]{:S(2)}, u32[]{:S(2)}) collective-permute-start(bf16[64,16,1,256]{3,1,2,0:T(8,128)(2,1)S(1)} %get-tuple-element.39), channel_id=1, source_target_pairs={{0,2},{2,4},{4,6},{6,8},{8,10},{10,12},{12,14},{1,3},{3,5},{5,7},{... | collective-permute-start | bytes 1572872 | tf_op jit(solution)/shard_map/ppermute | solution.py:26
  84.9 22.7 %collective-permute-start.5 = (bf16[64,16,1,256]{3,1,2,0:T(8,128)(2,1)S(1)}, bf16[64,16,1,256]{3,1,2,0:T(8,128)(2,1)S(1)}, u32[]{:S(2)}, u32[]{:S(2)}) collective-permute-start(bf16[64,16,1,256]{3,1,2,0:T(8,128)(2,1)S(1)} %get-tuple-element.40), channel_id=1, source_target_pairs={{2,0},{4,2},{6,4},{8,6},{10,8},{12,10},{14,12},{3,1},{5,3},{7,5},{... | collective-permute-start | bytes 1572872 | tf_op jit(solution)/shard_map/ppermute | solution.py:27
  107.6 2.8 %collective-permute-start.6 = (bf16[1,16,4,256]{3,1,2,0:T(8,128)(2,1)S(1)}, bf16[1,16,4,256]{3,1,2,0:T(8,128)(2,1)S(1)}, u32[]{:S(2)}, u32[]{:S(2)}) collective-permute-start(bf16[1,16,4,256]{3,1,2,0:T(8,128)(2,1)S(1)} %get-tuple-element.35), channel_id=1, source_target_pairs={{0,1},{2,3},{4,5},{6,7},{8,9},{10,11},{12,13},{14,15},{16,17},{18,... | collective-permute-start | bytes 98312 | tf_op jit(solution)/shard_map/ppermute | solution.py:26
  108.9 3.1 %collective-permute-start.7 = (bf16[1,16,4,256]{3,1,2,0:T(8,128)(2,1)S(1)}, bf16[1,16,4,256]{3,1,2,0:T(8,128)(2,1)S(1)}, u32[]{:S(2)}, u32[]{:S(2)}) collective-permute-start(bf16[1,16,4,256]{3,1,2,0:T(8,128)(2,1)S(1)} %get-tuple-element.36), channel_id=1, source_target_pairs={{1,0},{3,2},{5,4},{7,6},{9,8},{11,10},{13,12},{15,14},{17,16},{19,... | collective-permute-start | bytes 98312 | tf_op jit(solution)/shard_map/ppermute | solution.py:27
  118.3 1.4 copy-start.8
  118.3 1.4 copy-start.9
  119.7 9.8 %copy-start.4 = (f32[8,1024]{1,0:T(8,128)S(1)}, f32[8,1024]{1,0:T(8,128)}, u32[]{:S(2)}) copy-start(f32[8,1024]{1,0:T(8,128)} %param.19) | copy-start | bytes 98308
  123.8 25.6 %copy-start.3 = (f32[2,256]{1,0:T(2,128)}, f32[2,256]{1,0:T(2,128)S(1)}, u32[]{:S(2)}) copy-start(f32[2,256]{1,0:T(2,128)S(1)} %div.123) | copy-start | bytes 6148
  123.8 5.8 %collective-permute-start.8 = (f32[1,256]{1,0:T(1,128)S(1)}, f32[1,256]{1,0:T(1,128)S(1)}, u32[]{:S(2)}, u32[]{:S(2)}) collective-permute-start(f32[1,256]{1,0:T(1,128)S(1)} %get-tuple-element.52), channel_id=1, source_target_pairs={{0,2},{2,4},{4,6},{6,8},{8,10},{10,12},{12,14},{1,3},{3,5},{5,7},{... | collective-permute-start | bytes 3080 | tf_op jit(solution)/shard_map/ppermute | solution.py:26
  128.2 8.0 %collective-permute-start.9 = (f32[1,256]{1,0:T(1,128)S(1)}, f32[1,256]{1,0:T(1,128)S(1)}, u32[]{:S(2)}, u32[]{:S(2)}) collective-permute-start(f32[1,256]{1,0:T(1,128)S(1)} %get-tuple-element.53), channel_id=1, source_target_pairs={{2,0},{4,2},{6,4},{8,6},{10,8},{12,10},{14,12},{3,1},{5,3},{7,5},{... | collective-permute-start | bytes 3080 | tf_op jit(solution)/shard_map/ppermute | solution.py:27
  137.9 6.4 %collective-permute-start.10 = (bf16[2,8,1024]{2,1,0:T(8,128)(2,1)S(1)}, bf16[2,8,1024]{2,1,0:T(8,128)(2,1)S(1)}, u32[]{:S(2)}, u32[]{:S(2)}) collective-permute-start(bf16[2,8,1024]{2,1,0:T(8,128)(2,1)S(1)} %pad_maximum_fusion.8), channel_id=1, source_target_pairs={{0,2},{2,4},{4,6},{6,8},{8,10},{10,12},{12,14},{1,3},{3,5},{5,7},{... | collective-permute-start | bytes 98312 | tf_op jit(solution)/shard_map/ppermute | solution.py:26
  142.7 5.8 %collective-permute-start.11 = (bf16[2,8,1024]{2,1,0:T(8,128)(2,1)S(1)}, bf16[2,8,1024]{2,1,0:T(8,128)(2,1)S(1)}, u32[]{:S(2)}, u32[]{:S(2)}) collective-permute-start(bf16[2,8,1024]{2,1,0:T(8,128)(2,1)S(1)} %pad_maximum_fusion.8), channel_id=1, source_target_pairs={{2,0},{4,2},{6,4},{8,6},{10,8},{12,10},{14,12},{3,1},{5,3},{7,5},{... | collective-permute-start | bytes 98312 | tf_op jit(solution)/shard_map/ppermute | solution.py:27
where the time goes:
time: 153 us
  waiting for transfers between devices  56.4 us (37%)
  local copies, waits for them, and re-layouts  45.8 us (30%)
  starting transfers between devices  29.3 us (19%)
  matrix products  11.4 us (7%)
  other arithmetic  5.9 us (4%)
  blocking collectives  2.46 us (2%)
    ppermute x6, waiting for transfers between devices, with_halo(): before = lax.ppermute(last, axis, up)  42.3 us
    gather x2, local copies, waits for them, and re-layouts, take_plane(): return lax.dynamic_slice_in_dim(padded, DSP - plane, col_count, 2)  34.9 us
    ppermute x6, starting transfers between devices, with_halo(): before = lax.ppermute(last, axis, up)  21.1 us
    ppermute x6, waiting for transfers between devices, with_halo(): after = lax.ppermute(leading, axis, down)  14 us
    ppermute x6, starting transfers between devices, with_halo(): after = lax.ppermute(leading, axis, down)  8.15 us
    unnamed x43, local copies, waits for them, and re-layouts  5.54 us
    dot_general x4, matrix products, conv_valid(): jnp.einsum('dkrw,ko->dorw', columns[shift_d:shift_d + plane_total], folde...  5.53 us
  transfers between devices with their start and end apart: 12, of which 7 were waited for; matrix products, arithmetic and copies ran while one was open for 0% of the time, Pallas kernels for 0%

commit v1 on v0

v1 whole, which is shorter than its diff:
```python
import functools

import jax
import jax.numpy as jnp
from jax import lax
from jax.experimental import pallas as pl
from jax.experimental.pallas import tpu as pltpu
from jax.sharding import PartitionSpec as P

DSP = 128
UP = 4
TV_ITERS = 8
REACH = 2

dual_step = 0.175
primal_step = 0.7
tv_bound = 0.3
cost_scale = 8.0
mask_scale = 3.0
highest_prec = lax.Precision.HIGHEST
f32 = jnp.float32
bf16 = jnp.bfloat16
CHUNK1 = 11
CHUNK2 = 8


def iota(shape, dim):
    return lax.broadcasted_iota(jnp.int32, shape, dim)


def one_hot(cond):
    return jnp.where(cond, 1.0, 0.0)


def dot(a, b, dims=((1,), (0,)), precision=None):
    return lax.dot_general(a, b, (dims, ((), ())), precision=precision, preferred_element_type=f32)


def column(row, groups):
    ch = row.shape[1]
    shape = (groups * ch, ch)
    return jnp.sum(
        jnp.where(iota(shape, 0) % ch == iota(shape, 1), jnp.broadcast_to(row, shape), 0.0),
        axis=1,
        keepdims=True,
    )


def split(value):
    high = value.astype(bf16)
    return high, (value - high.astype(f32)).astype(bf16)


def kernel(
    npix, ndisp,
    left_ref, right_ref, featw_ref, w1_ref, b1_ref, w2_ref, b2_ref, head_ref, mask_ref, conf_ref,
    coarse_ref, out_ref,
    rows_buf, part_buf, wt_buf, wmat_buf, col_buf, lr_buf, hid_buf, score_buf, mix_buf,
    rows_send, rows_recv, part_send, part_recv,
):
    fine_rows, fine_cols = left_ref.shape
    rows = fine_rows // UP
    cols = fine_cols // UP
    ch = featw_ref.shape[1]
    planes = DSP // ndisp
    pix = lax.axis_index("pix")
    disp = lax.axis_index("disp")
    start = disp * planes

    def target(k, dc):
        return {"pix": pix + k, "disp": lax.rem(disp + dc, ndisp)}

    def exists(k):
        return (pix + k >= 0) & (pix + k < npix)

    offsets = [k for k in range(-REACH, REACH + 1)]
    barrier = pltpu.get_barrier_semaphore()
    expected = jnp.int32(0)
    for k in offsets:
        for dc in range(ndisp):
            if k == 0 and dc == 0:
                continue

            @pl.when(exists(k))
            def _():
                pl.semaphore_signal(
                    barrier, inc=1, device_id=target(k, dc), device_id_type=pl.DeviceIdType.MESH
                )

            expected = expected + jnp.where(exists(k), 1, 0)

    block = UP * (cols // UP)
    wide = block // UP
    ii, oo = iota((block, block), 0), iota((block, block), 1)
    undo = one_hot((ii % UP == oo // wide) & (ii // UP == oo % wide)).astype(bf16)
    stacked = jnp.concatenate(
        [
            (left_ref[...] - 128).astype(f32) / 64.0,
            (right_ref[...] - 128).astype(f32) / 64.0,
            conf_ref[...],
            jnp.zeros((fine_rows, fine_cols), f32),
        ],
        axis=0,
    ).astype(bf16)
    tall = stacked.shape[0]
    blocks = fine_cols // block
    res = dot(
        jnp.concatenate([stacked[:, j * block : (j + 1) * block] for j in range(blocks)], axis=0),
        undo,
    )
    by_b = [
        jnp.concatenate(
            [res[j * tall : (j + 1) * tall, b * wide : (b + 1) * wide] for j in range(blocks)],
            axis=1,
        )
        for b in range(UP)
    ]
    patch_left, patch_right, conf_rows = [
        jnp.concatenate([v[n * fine_rows : (n + 1) * fine_rows] for v in by_b], axis=0)
        for n in range(3)
    ]
    patch_rows = UP * fine_rows
    pp, qq = iota((UP * UP, patch_rows), 0), iota((UP * UP, patch_rows), 1)
    pick = one_hot(pp == UP * (qq % UP) + qq // fine_rows)
    spread = dot(featw_ref[...], pick, ((0,), (0,)), highest_prec)
    spread = jnp.concatenate([spread] * rows, axis=0)
    rr, qq = iota(spread.shape, 0), iota(spread.shape, 1)
    spread = jnp.where(rr // ch == (qq % fine_rows) // UP, spread, 0.0)
    frows = rows * ch
    rows_buf[1, 0:frows, :] = dot(spread, patch_left, precision=highest_prec).astype(bf16)
    rows_buf[1, frows : 2 * frows, :] = dot(spread, patch_right, precision=highest_prec).astype(bf16)
    rows_buf[1, 2 * frows : 2 * frows + patch_rows, :] = conf_rows.astype(bf16)

    pl.semaphore_wait(barrier, expected)

    def rows_copy(k):
        return pltpu.make_async_remote_copy(
            src_ref=rows_buf.at[1],
            dst_ref=rows_buf.at[1 - k],
            send_sem=rows_send.at[1 + k],
            recv_sem=rows_recv.at[1 - k],
            device_id=target(k, 0),
            device_id_type=pl.DeviceIdType.MESH,
        )

    for k in (-1, 1):

        @pl.when(exists(k))
        def _():
            rows_copy(k).start()

        @pl.when(jnp.logical_not(exists(k)))
        def _():
            rows_buf[1 + k] = jnp.zeros(rows_buf.shape[1:], bf16)

    for n, w_ref in enumerate((w1_ref, w2_ref)):
        wt_buf[...] = jnp.zeros_like(wt_buf)
        for kd in range(3):
            for ky in range(3):
                for kx in range(3):
                    tap = w_ref[kd, ky, kx].astype(f32)
                    for pd in range(2):
                        for py in range(2):
                            row = ((kd + pd) * 4 + ky + py) * ch
                            col = (kx * 4 + pd * 2 + py) * ch
                            wt_buf[row : row + ch, col : col + ch] = tap
        wmat_buf[n] = wt_buf[...].T[: 12 * ch].astype(bf16)
    group = 4 * ch
    for n, ref in enumerate((b1_ref, b2_ref, head_ref)):
        col_buf[n] = jnp.broadcast_to(column(ref[...], 4), (group, cols))

    def rows_wait(k):
        return pltpu.make_async_remote_copy(
            src_ref=rows_buf.at[1],
            dst_ref=rows_buf.at[1 + k],
            send_sem=rows_send.at[1 + k],
            recv_sem=rows_recv.at[1 + k],
            device_id=target(k, 0),
            device_id_type=pl.DeviceIdType.MESH,
        )

    for k in (-1, 1):

        @pl.when(exists(k))
        def _():
            rows_wait(k).wait_recv()

    for slot in range(3):
        for side in range(2):
            lr_buf[side, slot * frows : (slot + 1) * frows, :] = rows_buf[
                slot, side * frows : (side + 1) * frows, :
            ].astype(f32)

    lane = iota((group, cols), 1)
    not_first = lane >= 1
    not_last = lane < cols - 1

    def conv(weights, values):
        acc = dot(weights, values)
        before = jnp.where(not_first, pltpu.roll(acc[0:group], 1, 1), 0.0)
        after = jnp.where(not_last, pltpu.roll(acc[2 * group :], cols - 1, 1), 0.0)
        return acc[group : 2 * group] + before + after

    def volume(plane):
        shift = lax.rem(plane + cols, cols)
        moved = pltpu.roll(lr_buf[1], shift, 1)
        keep = (iota(moved.shape, 1) >= plane) & (plane >= 0) & (plane < DSP)
        return jnp.where(keep, moved * lr_buf[0], 0.0).astype(bf16)

    vrows = 4 * ch
    half = 2 * ch

    def first(c, carry):
        base = c * (2 * CHUNK1)
        held = [volume(start - 2 + base), volume(start - 1 + base)]
        for j in range(CHUNK1):
            held = held[-2:] + [volume(start + base + 2 * j + n) for n in range(2)]
            for rb in range(2):
                values = jnp.concatenate([v[rb * half : rb * half + vrows] for v in held], axis=0)
                got = jnp.maximum(conv(wmat_buf[0], values) + col_buf[0], 0.0).astype(bf16)
                for pd in range(2):
                    hid_buf[base + 2 * j + pd, rb * half : (rb + 1) * half, :] = got[
                        pd * half : (pd + 1) * half
                    ]
        return carry

    lax.fori_loop(0, (planes // 2 + 1) // CHUNK1, first, 0)

    @pl.when(pix == 0)
    def _():
        hid_buf[:, 0:ch, :] = jnp.zeros((planes + 2, ch, cols), bf16)

    @pl.when(pix == npix - 1)
    def _():
        hid_buf[:, 3 * ch : 4 * ch, :] = jnp.zeros((planes + 2, ch, cols), bf16)

    @pl.when(disp == 0)
    def _():
        hid_buf[0] = jnp.zeros((4 * ch, cols), bf16)

    @pl.when(disp == ndisp - 1)
    def _():
        hid_buf[planes + 1] = jnp.zeros((4 * ch, cols), bf16)

    def second(c, carry):
        base = c * CHUNK2
        for j in range(CHUNK2):
            values = hid_buf[pl.ds(2 * (base + j), 4)].reshape(4 * vrows, cols)
            got = jnp.maximum(conv(wmat_buf[1], values) + col_buf[1], 0.0) * col_buf[2]
            score_buf[base + j] = jnp.sum(got.reshape(4, ch, cols), axis=1)
        return carry

    lax.fori_loop(0, planes // 2 // CHUNK2, second, 0)

    expo = jnp.exp(-cost_scale * jnp.tanh(score_buf[...]))
    shape = expo.shape
    plane = start + 2 * iota(shape, 0) + iota(shape, 1) // rows
    weight4 = jnp.sum(expo, axis=0)
    plane4 = jnp.sum(expo * (plane.astype(f32) / DSP), axis=0)
    mine = jnp.concatenate(
        [plane4[0:rows] + plane4[rows:], weight4[0:rows] + weight4[rows:], jnp.ones((4, cols), f32)],
        axis=0,
    )
    part_buf[REACH, disp] = mine

    def part_copy(k, dc):
        return pltpu.make_async_remote_copy(
            src_ref=part_buf.at[REACH, disp],
            dst_ref=part_buf.at[REACH - k, disp],
            send_sem=part_send.at[REACH + k, dc],
            recv_sem=part_recv.at[REACH - k, disp],
            device_id=target(k, dc),
            device_id_type=pl.DeviceIdType.MESH,
        )

    def part_wait(k, dc):
        core = lax.rem(disp + dc, ndisp)
        return pltpu.make_async_remote_copy(
            src_ref=part_buf.at[REACH, disp],
            dst_ref=part_buf.at[REACH + k, core],
            send_sem=part_send.at[REACH + k, dc],
            recv_sem=part_recv.at[REACH + k, core],
            device_id=target(k, dc),
            device_id_type=pl.DeviceIdType.MESH,
        )

    partners = [(k, dc) for k in (2, -2, 1, -1, 0) for dc in range(ndisp) if (k, dc) != (0, 0)]
    for k, dc in partners:

        @pl.when(exists(k))
        def _():
            part_copy(k, dc).start()

    for k in (-2, -1, 1, 2):

        @pl.when(jnp.logical_not(exists(k)))
        def _():
            for core in range(ndisp):
                part_buf[REACH + k, core] = jnp.where(iota((8, cols), 0) < rows, 0.0, 1.0)

    deep = 8
    taps = mask_ref.shape[1]
    cc, qq = iota((ch, deep * ch), 0), iota((ch, deep * ch), 1)
    tiled = dot(mask_ref[...], one_hot(cc == qq % ch), ((0,), (0,)), highest_prec)
    shape = (taps, deep, deep * ch)
    big = jnp.where(
        iota(shape, 1) == iota(shape, 2) // ch, jnp.broadcast_to(tiled[:, None, :], shape), 0.0
    ).reshape(taps * deep, deep * ch)
    none = jnp.zeros((ch, cols), bf16)
    lines = jnp.concatenate(
        [none] + [rows_buf[slot, 0:frows, :] for slot in range(3)] + [none], axis=0
    )
    big_high, big_low = split(big)
    logits = dot(
        jnp.concatenate([big_high, big_low], axis=1), jnp.concatenate([lines, lines], axis=0)
    )
    expo = jnp.exp(mask_scale * jnp.tanh(logits)).reshape(9, UP * UP, deep, cols)
    mix_buf[...] = expo * (1.0 / jnp.sum(expo, axis=0))[None]

    conf_all = jnp.concatenate(
        [rows_buf[slot, 2 * frows : 2 * frows + patch_rows, :] for slot in range(3)], axis=0
    )
    shape = (UP * UP * deep, 3 * patch_rows)
    to, fr = iota(shape, 0), iota(shape, 1)
    to_a, to_b, to_s = to // (UP * deep), (to // deep) % UP, to % deep
    fr_slot, fr_b, fr_r, fr_a = fr // patch_rows, (fr // fine_rows) % UP, (fr // UP) % rows, fr % UP
    place = one_hot((to_a == fr_a) & (to_b == fr_b) & (to_s - 1 == fr_slot * rows + fr_r))
    fidelity = dot(place.astype(bf16), conf_all).reshape(UP, UP, deep, cols)
    inverse = 1.0 / (1.0 + primal_step * fidelity)

    for k, dc in partners:

        @pl.when(exists(k))
        def _():
            part_wait(k, dc).wait_recv()

    total = part_buf[:, 0]
    for core in range(1, ndisp):
        total = total + part_buf[:, core]
    ratio = [total[n][0:rows] / total[n][rows : 2 * rows] for n in range(2 * REACH + 1)]
    coarse_ref[...] = ratio[REACH]
    coarse = jnp.concatenate([ratio[0][1:2]] + ratio[1:-1] + [ratio[-1][0:1]], axis=0)

    lane8 = iota((deep, cols), 1)
    lane_first, lane_last = lane8 >= 1, lane8 < cols - 1
    initial = None
    for ky in range(3):
        line = coarse if ky == 1 else pltpu.roll(coarse, (1 - ky) % deep, 0)
        for kx in range(3):
            if kx == 0:
                near = jnp.where(lane_first, pltpu.roll(line, 1, 1), 0.0)
            elif kx == 2:
                near = jnp.where(lane_last, pltpu.roll(line, cols - 1, 1), 0.0)
            else:
                near = line
            term = mix_buf[3 * ky + kx] * near[None]
            initial = term if initial is None else initial + term
    initial = initial.reshape(UP, UP, deep, cols)
    constant = primal_step * fidelity * initial * inverse

    line = pix * rows - 3 + iota((deep, cols), 0)
    inside = (line >= 0) & (line < npix * rows)
    inside_last = (line >= 0) & (line < npix * rows - 1)

    def tv(step, current):
        primal, extrap, dual_x, dual_y = current
        over = [
            jnp.where(lane_last, pltpu.roll(extrap[a, 0], cols - 1, 1) - extrap[a, UP - 1], 0.0)
            for a in range(UP)
        ]
        grad_x = jnp.concatenate(
            [extrap[:, 1:] - extrap[:, :-1], jnp.stack(over)[:, None]], axis=1
        )
        under = [
            jnp.where(inside_last, pltpu.roll(extrap[0, b], deep - 1, 0) - extrap[UP - 1, b], 0.0)
            for b in range(UP)
        ]
        grad_y = jnp.concatenate(
            [jnp.where(inside[None, None], extrap[1:] - extrap[:-1], 0.0), jnp.stack(under)[None]],
            axis=0,
        )
        trial_x = dual_x + dual_step * grad_x
        trial_y = dual_y + dual_step * grad_y
        square = jnp.maximum(trial_x * trial_x + trial_y * trial_y, 1e-30)
        shrink = jnp.minimum(1.0, tv_bound * lax.rsqrt(square))
        dual_x = trial_x * shrink
        dual_y = trial_y * shrink
        prior = [
            jnp.where(lane_first, pltpu.roll(dual_x[a, UP - 1], 1, 1), 0.0) for a in range(UP)
        ]
        left = jnp.concatenate([jnp.stack(prior)[:, None], dual_x[:, :-1]], axis=1)
        above = [pltpu.roll(dual_y[UP - 1, b], 1, 0) for b in range(UP)]
        upper = jnp.concatenate([jnp.stack(above)[None], dual_y[:-1]], axis=0)
        divergence = dual_x - left + dual_y - upper
        updated = (primal + primal_step * divergence) * inverse + constant
        return (updated, 2.0 * updated - primal, dual_x, dual_y)

    zeros = jnp.zeros_like(initial)
    result = lax.fori_loop(0, TV_ITERS, tv, (initial, initial, zeros, zeros))[0]

    shape = (fine_rows, UP * deep)
    to, fr = iota(shape, 0), iota(shape, 1)
    own = one_hot((to % UP == fr // deep) & (to // UP + 3 == fr % deep)).astype(bf16)
    pieces = []
    for b in range(UP):
        high, low = split(result[:, b].reshape(UP * deep, cols))
        pieces.append(jnp.concatenate([dot(own, high), dot(own, low)], axis=0).astype(bf16))
    redo = one_hot((oo % UP == ii // wide) & (oo // UP == ii % wide)).astype(bf16)
    for j in range(blocks):
        packed = jnp.concatenate([v[:, j * wide : (j + 1) * wide] for v in pieces], axis=1)
        both = dot(packed, redo)
        out_ref[:, j * block : (j + 1) * block] = both[0:fine_rows] + both[fine_rows:]

    for k in (-1, 1):

        @pl.when(exists(k))
        def _():
            rows_copy(k).wait_send()

    for k, dc in partners:

        @pl.when(exists(k))
        def _():
            part_copy(k, dc).wait_send()


def local(
    left_image, right_image, feat_weight, first_weight, first_bias,
    second_weight, second_bias, head_weight, mask_weight, confidence,
):
    npix, ndisp = lax.axis_size("pix"), lax.axis_size("disp")
    fine_rows, fine_cols = left_image.shape
    rows, cols = fine_rows // UP, fine_cols // UP
    ch = feat_weight.shape[1]
    planes = DSP // ndisp
    assert fine_rows == TV_ITERS and rows == 2
    vmem = pl.BlockSpec(memory_space=pltpu.VMEM)
    return pl.pallas_call(
        functools.partial(kernel, npix, ndisp),
        out_shape=(
            jax.ShapeDtypeStruct((rows, cols), f32),
            jax.ShapeDtypeStruct((fine_rows, fine_cols), f32),
        ),
        in_specs=[vmem] * 10,
        out_specs=(vmem, vmem),
        scratch_shapes=[
            pltpu.VMEM((3, 2 * rows * ch + UP * fine_rows, cols), bf16),
            pltpu.VMEM((2 * REACH + 1, ndisp, 8, cols), f32),
            pltpu.VMEM((16 * ch, 16 * ch), f32),
            pltpu.VMEM((2, 12 * ch, 16 * ch), bf16),
            pltpu.VMEM((3, 4 * ch, cols), f32),
            pltpu.VMEM((2, 3 * rows * ch, cols), f32),
            pltpu.VMEM((planes + 2, 4 * ch, cols), bf16),
            pltpu.VMEM((planes // 2, 2 * rows, cols), f32),
            pltpu.VMEM((9, UP * UP, 8, cols), f32),
            pltpu.SemaphoreType.DMA((3,)),
            pltpu.SemaphoreType.DMA((3,)),
            pltpu.SemaphoreType.DMA((2 * REACH + 1, ndisp)),
            pltpu.SemaphoreType.DMA((2 * REACH + 1, ndisp)),
        ],
        compiler_params=pltpu.CompilerParams(
            collective_id=0, has_side_effects=True, vmem_limit_bytes=40 * 1024 * 1024
        ),
    )(
        left_image, right_image, feat_weight, first_weight, first_bias[None],
        second_weight, second_bias[None], head_weight[None], mask_weight, confidence,
    )


def solution(mesh):
    placed = (
        P(("grp", "pix"), None),
        P(("grp", "pix"), None),
        P(),
        P(),
        P(),
        P(),
        P(),
        P(),
        P(),
        P(("grp", "pix"), None),
    )
    return jax.shard_map(
        local,
        mesh=mesh,
        in_specs=placed,
        out_specs=(P(("grp", "pix"), None), P(("grp", "pix"), None)),
        check_vma=False,
    )
```

time: 153 us -> 33.2 us (0.22)
  waiting for transfers between devices: 56.4 us -> 0 us
  local copies, waits for them, and re-layouts: 45.8 us -> 7.34 us
  starting transfers between devices: 29.3 us -> 0 us
  Pallas kernels: 0 us -> 24.7 us
  matrix products: 11.4 us -> 0 us
  other arithmetic: 5.9 us -> 0 us
  blocking collectives: 2.46 us -> 0 us
    ppermute x12 -> x0, waiting for transfers between devices: 56.4 us -> none  [the longest x6 42.3 us: with_halo(): before = lax.ppermute(last, axis, up)]
    gather x2 -> x0, local copies, waits for them, and re-layouts: 34.9 us -> none  [take_plane(): return lax.dynamic_slice_in_dim(padded, DSP - plane, col_count, 2)]
    ppermute x12 -> x0, starting transfers between devices: 29.3 us -> none  [the longest x6 21.1 us: with_halo(): before = lax.ppermute(last, axis, up)]
    pallas_call x0 -> x1, Pallas kernels: none -> 24.7 us  [local(): pl.pallas_call(functools.partial(kernel, npix, ndisp), out_shape=(jax.Sha...]
    dot_general x10 -> x0, matrix products: 11.4 us -> none  [the longest x4 5.53 us: conv_valid(): jnp.einsum('dkrw,ko->dorw', columns[shift_d:shift_d + plane_total], folde...]
    psum x1 -> x0, blocking collectives: 2.46 us -> none  [local(): lax.psum((jnp.sum(expo, 0), jnp.sum(expo * plane_frac[:, None, None], 0))...]
    sub x18 -> x0, other arithmetic: 2.34 us -> none  [the longest x2 0.77 us: features(): pixels = image.astype(jnp.float32) / 64.0 - 2.0]
    div x17 -> x0, other arithmetic: 2.14 us -> none  [the longest x8 1.1 us: tv_iter(): dual_x = trial_x / shrink]
  transfers between devices with their start and end apart: 12 -> 0, of which waited for: 7 -> 0; matrix products, arithmetic and copies ran while one was open for 0% -> 0% of each run, Pallas kernels for 0% -> 0%
where the time goes in v1:
time: 33.2 us; the launch traced here: 32.7 us
  Pallas kernels  24.7 us (74%)
  local copies, waits for them, and re-layouts  7.34 us (22%)
  between operations  0.67 us (2%)
    pallas_call x1, Pallas kernels, local(): pl.pallas_call(functools.partial(kernel, npix, ndisp), out_shape=(jax.Sha...  24.7 us
    unnamed x22, local copies, waits for them, and re-layouts  7.34 us

profile of v1, /device:TPU:0, one launch (start us, length us, event | category | flops | bytes accessed | tf_op | source)
XLA Modules:
  0.0 32.7 jit_solution(3480606488129331245)
XLA Ops:
  0.6 0.0 copy-start.7
  0.6 0.0 copy-start.8
  0.7 0.0 copy-start.9
  0.7 0.6 %copy-done.7 = f32[16]{0:T(128)S(1)} copy-done((f32[16]{0:T(128)S(1)}, f32[16]{0:T(128)}, u32[]{:S(2)}) %copy-start.7) | copy-done | bytes 88
  1.3 0.0 copy-done.8
  1.3 0.0 copy-done.9
  1.3 0.0 copy-start
  1.3 0.9 %copy-done = bf16[3,3,3,16,16]{4,3,2,1,0:T(8,128)(2,1)S(1)} copy-done((bf16[3,3,3,16,16]{4,3,2,1,0:T(8,128)(2,1)S(1)}, bf16[3,3,3,16,16]{4,3,2,1,0:T(8,128)(2,1)}, u32[]{:S(2)}) %copy-start) | copy-done | bytes 13848
  2.2 0.0 copy-start.1
  2.2 0.9 %copy-done.1 = bf16[3,3,3,16,16]{4,3,2,1,0:T(8,128)(2,1)S(1)} copy-done((bf16[3,3,3,16,16]{4,3,2,1,0:T(8,128)(2,1)S(1)}, bf16[3,3,3,16,16]{4,3,2,1,0:T(8,128)(2,1)}, u32[]{:S(2)}) %copy-start.1) | copy-done | bytes 13848
  3.1 0.0 copy-start.2
  3.1 0.8 %copy-done.2 = s32[8,1024]{1,0:T(8,128)S(1)} copy-done((s32[8,1024]{1,0:T(8,128)S(1)}, s32[8,1024]{1,0:T(8,128)}, u32[]{:S(2)}) %copy-start.2) | copy-done | bytes 32792
  3.9 0.0 copy-start.3
  3.9 0.8 %copy-done.3 = s32[8,1024]{1,0:T(8,128)S(1)} copy-done((s32[8,1024]{1,0:T(8,128)S(1)}, s32[8,1024]{1,0:T(8,128)}, u32[]{:S(2)}) %copy-start.3) | copy-done | bytes 32792
  4.6 0.0 copy-start.4
  4.6 0.8 %copy-done.4 = f32[8,1024]{1,0:T(8,128)S(1)} copy-done((f32[8,1024]{1,0:T(8,128)S(1)}, f32[8,1024]{1,0:T(8,128)}, u32[]{:S(2)}) %copy-start.4) | copy-done | bytes 32792
  5.4 0.0 copy-start.5
  5.4 0.7 %copy-done.5 = f32[16,144]{1,0:T(8,128)S(1)} copy-done((f32[16,144]{1,0:T(8,128)S(1)}, f32[16,144]{1,0:T(8,128)}, u32[]{:S(2)}) %copy-start.5) | copy-done | bytes 9240
  6.1 0.0 copy-start.6
  6.1 0.7 %copy-done.6 = f32[16,16]{1,0:T(8,128)S(1)} copy-done((f32[16,16]{1,0:T(8,128)S(1)}, f32[16,16]{1,0:T(8,128)}, u32[]{:S(2)}) %copy-start.6) | copy-done | bytes 1048
  6.8 24.7 %shard_map.113 = (f32[2,256]{1,0:T(2,128)S(1)}, f32[8,1024]{1,0:T(8,128)S(1)}) custom-call(s32[8,1024]{1,0:T(8,128)S(1)} %copy-done.2, s32[8,1024]{1,0:T(8,128)S(1)} %copy-done.3, f32[16,16]{1,0:T(8,128)S(1)} %copy-done.6, bf16[3,3,3,16,16]{4,3,2,1,0:T(8,128)(2,1)S(1)} %copy-done, f32[1,16]{1,0:T(1,128)S(1)} %bitcast.3, ...), custom_call_target="tpu_custom_call" | custom-call | tf_op jit(solution)/shard_map/pallas_call | solution.py:438
  31.5 0.6 %copy.14 = f32[2,256]{1,0:T(2,128)} copy(f32[2,256]{1,0:T(2,128)S(1)} %get-tuple-element.4) | data formatting | bytes 4096
  32.1 0.6 %copy.15 = f32[8,1024]{1,0:T(8,128)} copy(f32[8,1024]{1,0:T(8,128)S(1)} %get-tuple-element.5) | data formatting | bytes 65536
Async XLA Ops:
  0.6 0.7 %copy-start.7 = (f32[16]{0:T(128)S(1)}, f32[16]{0:T(128)}, u32[]{:S(2)}) copy-start(f32[16]{0:T(128)} %param.14) | copy-start | bytes 196
  0.6 0.7 %copy-start.8 = (f32[16]{0:T(128)S(1)}, f32[16]{0:T(128)}, u32[]{:S(2)}) copy-start(f32[16]{0:T(128)} %param.16) | copy-start | bytes 196
  0.7 0.7 %copy-start.9 = (f32[16]{0:T(128)S(1)}, f32[16]{0:T(128)}, u32[]{:S(2)}) copy-start(f32[16]{0:T(128)} %param.17) | copy-start | bytes 196
  1.3 0.9 %copy-start = (bf16[3,3,3,16,16]{4,3,2,1,0:T(8,128)(2,1)S(1)}, bf16[3,3,3,16,16]{4,3,2,1,0:T(8,128)(2,1)}, u32[]{:S(2)}) copy-start(bf16[3,3,3,16,16]{4,3,2,1,0:T(8,128)(2,1)} %w1_ref.1) | copy-start | bytes 41476
  2.2 0.9 %copy-start.1 = (bf16[3,3,3,16,16]{4,3,2,1,0:T(8,128)(2,1)S(1)}, bf16[3,3,3,16,16]{4,3,2,1,0:T(8,128)(2,1)}, u32[]{:S(2)}) copy-start(bf16[3,3,3,16,16]{4,3,2,1,0:T(8,128)(2,1)} %w2_ref.1) | copy-start | bytes 41476
  3.1 0.8 %copy-start.2 = (s32[8,1024]{1,0:T(8,128)S(1)}, s32[8,1024]{1,0:T(8,128)}, u32[]{:S(2)}) copy-start(s32[8,1024]{1,0:T(8,128)} %left_ref.1) | copy-start | bytes 98308
  3.9 0.8 %copy-start.3 = (s32[8,1024]{1,0:T(8,128)S(1)}, s32[8,1024]{1,0:T(8,128)}, u32[]{:S(2)}) copy-start(s32[8,1024]{1,0:T(8,128)} %right_ref.1) | copy-start | bytes 98308
  4.6 0.8 %copy-start.4 = (f32[8,1024]{1,0:T(8,128)S(1)}, f32[8,1024]{1,0:T(8,128)}, u32[]{:S(2)}) copy-start(f32[8,1024]{1,0:T(8,128)} %conf_ref.1) | copy-start | bytes 98308
  5.4 0.7 %copy-start.5 = (f32[16,144]{1,0:T(8,128)S(1)}, f32[16,144]{1,0:T(8,128)}, u32[]{:S(2)}) copy-start(f32[16,144]{1,0:T(8,128)} %mask_ref.1) | copy-start | bytes 27652
  6.1 0.7 %copy-start.6 = (f32[16,16]{1,0:T(8,128)S(1)}, f32[16,16]{1,0:T(8,128)}, u32[]{:S(2)}) copy-start(f32[16,16]{1,0:T(8,128)} %featw_ref.1) | copy-start | bytes 3076

commit v2 on v1

--- a/solution.py
+++ b/solution.py
@@ -20,6 +20,7 @@
 highest_prec = lax.Precision.HIGHEST
 f32 = jnp.float32
 bf16 = jnp.bfloat16
+LANES = 128
 CHUNK1 = 11
 CHUNK2 = 8
 
@@ -53,9 +54,11 @@
 
 def kernel(
     npix, ndisp,
+    left_hbm, right_hbm, featw_hbm, w1_hbm, b1_hbm, w2_hbm, b2_hbm, head_hbm, mask_hbm, conf_hbm,
+    coarse_ref, out_ref,
     left_ref, right_ref, featw_ref, w1_ref, b1_ref, w2_ref, b2_ref, head_ref, mask_ref, conf_ref,
-    coarse_ref, out_ref,
-    rows_buf, part_buf, wt_buf, wmat_buf, col_buf, lr_buf, hid_buf, score_buf, mix_buf,
+    load_sem,
+    keep_buf, rows_buf, part_buf, wt_buf, wmat_buf, col_buf, lr_buf, hid_buf, score_buf, mix_buf,
     rows_send, rows_recv, part_send, part_recv,
 ):
     fine_rows, fine_cols = left_ref.shape
@@ -73,6 +76,26 @@
     def exists(k):
         return (pix + k >= 0) & (pix + k < npix)
 
+    loads = [
+        pltpu.make_async_copy(src, dst, load_sem.at[n])
+        for n, (src, dst) in enumerate(
+            (
+                (left_hbm, left_ref),
+                (right_hbm, right_ref),
+                (conf_hbm, conf_ref),
+                (featw_hbm, featw_ref),
+                (w1_hbm, w1_ref),
+                (w2_hbm, w2_ref),
+                (b1_hbm, b1_ref),
+                (b2_hbm, b2_ref),
+                (head_hbm, head_ref),
+                (mask_hbm, mask_ref),
+            )
+        )
+    ]
+    for load in loads:
+        load.start()
+
     offsets = [k for k in range(-REACH, REACH + 1)]
     barrier = pltpu.get_barrier_semaphore()
     expected = jnp.int32(0)
@@ -93,6 +116,8 @@
     wide = block // UP
     ii, oo = iota((block, block), 0), iota((block, block), 1)
     undo = one_hot((ii % UP == oo // wide) & (ii // UP == oo % wide)).astype(bf16)
+    for load in loads[:4]:
+        load.wait()
     stacked = jnp.concatenate(
         [
             (left_ref[...] - 128).astype(f32) / 64.0,
@@ -153,6 +178,9 @@
         def _():
             rows_buf[1 + k] = jnp.zeros(rows_buf.shape[1:], bf16)
 
+    for load in loads[4:]:
+        load.wait()
+
     for n, w_ref in enumerate((w1_ref, w2_ref)):
         wt_buf[...] = jnp.zeros_like(wt_buf)
         for kd in range(3):
@@ -191,15 +219,24 @@
                 slot, side * frows : (side + 1) * frows, :
             ].astype(f32)
 
-    lane = iota((group, cols), 1)
+    lane = iota((group, LANES), 1)
     not_first = lane >= 1
-    not_last = lane < cols - 1
+    not_last = lane < LANES - 1
 
     def conv(weights, values):
         acc = dot(weights, values)
-        before = jnp.where(not_first, pltpu.roll(acc[0:group], 1, 1), 0.0)
-        after = jnp.where(not_last, pltpu.roll(acc[2 * group :], cols - 1, 1), 0.0)
-        return acc[group : 2 * group] + before + after
+        moved_right, moved_left = {}, {}
+        parts = []
+        for n in range(cols // LANES):
+            at = slice(n * LANES, (n + 1) * LANES)
+            moved_right[n] = pltpu.roll(acc[0:group, at], 1, 1)
+            moved_left[n] = pltpu.roll(acc[2 * group :, at], LANES - 1, 1)
+        for n in range(cols // LANES):
+            at = slice(n * LANES, (n + 1) * LANES)
+            before = jnp.where(not_first, moved_right[n], moved_right.get(n - 1, 0.0))
+            after = jnp.where(not_last, moved_left[n], moved_left.get(n + 1, 0.0))
+            parts.append(acc[group : 2 * group, at] + before + after)
+        return jnp.concatenate(parts, axis=1)
 
     def volume(plane):
         shift = lax.rem(plane + cols, cols)
@@ -210,11 +247,18 @@
     vrows = 4 * ch
     half = 2 * ch
 
+    left_rows = lr_buf[0].astype(bf16)
+    keep_buf[...] = one_hot(iota(keep_buf.shape, 1) >= 1).astype(bf16)
+
     def first(c, carry):
         base = c * (2 * CHUNK1)
-        held = [volume(start - 2 + base), volume(start - 1 + base)]
+        held, moved = list(carry[:2]), carry[2]
         for j in range(CHUNK1):
-            held = held[-2:] + [volume(start + base + 2 * j + n) for n in range(2)]
+            held = held[-2:]
+            for n in range(2):
+                held.append(moved * left_rows)
+                inside = (start + base + 2 * j + n + 1 < DSP).astype(f32).astype(bf16)
+                moved = pltpu.roll(moved, 1, 1) * (keep_buf[...] * inside)
             for rb in range(2):
                 values = jnp.concatenate([v[rb * half : rb * half + vrows] for v in held], axis=0)
                 got = jnp.maximum(conv(wmat_buf[0], values) + col_buf[0], 0.0).astype(bf16)
@@ -222,9 +266,17 @@
                     hid_buf[base + 2 * j + pd, rb * half : (rb + 1) * half, :] = got[
                         pd * half : (pd + 1) * half
                     ]
-        return carry
-
-    lax.fori_loop(0, (planes // 2 + 1) // CHUNK1, first, 0)
+        return (held[-2], held[-1], moved)
+
+    opening = jnp.where(
+        iota(lr_buf.shape[1:], 1) >= start, pltpu.roll(lr_buf[1], start, 1), 0.0
+    ).astype(bf16)
+    lax.fori_loop(
+        0,
+        (planes // 2 + 1) // CHUNK1,
+        first,
+        (volume(start - 2), volume(start - 1), opening),
+    )
 
     @pl.when(pix == 0)
     def _():
@@ -435,15 +487,22 @@
     planes = DSP // ndisp
     assert fine_rows == TV_ITERS and rows == 2
     vmem = pl.BlockSpec(memory_space=pltpu.VMEM)
+    args = (
+        left_image, right_image, feat_weight, first_weight, first_bias[None],
+        second_weight, second_bias[None], head_weight[None], mask_weight, confidence,
+    )
     return pl.pallas_call(
         functools.partial(kernel, npix, ndisp),
         out_shape=(
             jax.ShapeDtypeStruct((rows, cols), f32),
             jax.ShapeDtypeStruct((fine_rows, fine_cols), f32),
         ),
-        in_specs=[vmem] * 10,
+        in_specs=[pl.BlockSpec(memory_space=pltpu.HBM)] * 10,
         out_specs=(vmem, vmem),
-        scratch_shapes=[
+        scratch_shapes=[pltpu.VMEM(arg.shape, arg.dtype) for arg in args]
+        + [
+            pltpu.SemaphoreType.DMA((len(args),)),
+            pltpu.VMEM((3 * rows * ch, cols), bf16),
             pltpu.VMEM((3, 2 * rows * ch + UP * fine_rows, cols), bf16),
             pltpu.VMEM((2 * REACH + 1, ndisp, 8, cols), f32),
             pltpu.VMEM((16 * ch, 16 * ch), f32),
@@ -459,12 +518,9 @@
             pltpu.SemaphoreType.DMA((2 * REACH + 1, ndisp)),
         ],
         compiler_params=pltpu.CompilerParams(
-            collective_id=0, has_side_effects=True, vmem_limit_bytes=40 * 1024 * 1024
+            collective_id=0, has_side_effects=True, vmem_limit_bytes=56 * 1024 * 1024
         ),
-    )(
-        left_image, right_image, feat_weight, first_weight, first_bias[None],
-        second_weight, second_bias[None], head_weight[None], mask_weight, confidence,
-    )
+    )(*args)
 
 
 def solution(mesh):

time: 33.2 us -> 26.1 us (0.79)
  local copies, waits for them, and re-layouts: 7.34 us -> 2.6 us
  Pallas kernels: 24.7 us -> 22.6 us
    unnamed x22 -> x4, local copies, waits for them, and re-layouts: 7.34 us -> 2.6 us
    pallas_call x1, Pallas kernels: 24.7 us -> 22.6 us  [local(): pl.pallas_call(functools.partial(kernel, npix, ndisp), out_shape=(jax.Sha...]
where the time goes in v2:
time: 26.1 us; the launch traced here: 25.9 us
  Pallas kernels  22.6 us (87%)
  local copies, waits for them, and re-layouts  2.6 us (10%)
  between operations  0.65 us (2%)
    pallas_call x1, Pallas kernels, local(): pl.pallas_call(functools.partial(kernel, npix, ndisp), out_shape=(jax.Sha...  22.6 us
    unnamed x4, local copies, waits for them, and re-layouts  2.6 us

profile of v2, /device:TPU:0, one launch (start us, length us, event | category | flops | bytes accessed | tf_op | source)
XLA Modules:
  0.0 25.9 jit_solution(10975400589732521320)
XLA Ops:
  0.6 22.6 %shard_map.113 = (f32[2,256]{1,0:T(2,128)}, f32[8,1024]{1,0:T(8,128)}) custom-call(s32[8,1024]{1,0:T(8,128)} %left_hbm.1, s32[8,1024]{1,0:T(8,128)} %right_hbm.1, f32[16,16]{1,0:T(8,128)} %featw_hbm.1, bf16[3,3,3,16,16]{4,3,2,1,0:T(8,128)(2,1)} %w1_hbm.1, f32[1,16]{1,0:T(1,128)} %bitcast.3, bf16[3,3,3,16,16]{4,3,2,1,0:T(8,128)(2,1)} %w2_hbm.1, ...), custom_call_target="tpu_custom_call" | custom-call | tf_op jit(solution)/shard_map/pallas_call | solution.py:494
  23.3 0.0 copy-start
  23.3 0.6 %copy-done = f32[2,256]{1,0:T(2,128)S(1)} copy-done((f32[2,256]{1,0:T(2,128)S(1)}, f32[2,256]{1,0:T(2,128)}, u32[]{:S(2)}) %copy-start) | copy-done | bytes 2072
  23.9 0.6 %copy.14 = f32[2,256]{1,0:T(2,128)} copy(f32[2,256]{1,0:T(2,128)S(1)} %copy-done) | data formatting | bytes 4096
  24.5 1.4 %copy.15 = f32[8,1024]{1,0:T(8,128)} copy(f32[8,1024]{1,0:T(8,128)} %get-tuple-element.5) | data formatting | bytes 65536
Async XLA Ops:
  23.3 0.7 %copy-start = (f32[2,256]{1,0:T(2,128)S(1)}, f32[2,256]{1,0:T(2,128)}, u32[]{:S(2)}) copy-start(f32[2,256]{1,0:T(2,128)} %get-tuple-element.4) | copy-start | bytes 6148

commit v3 on v2

--- a/solution.py
+++ b/solution.py
@@ -408,10 +408,10 @@
             term = mix_buf[3 * ky + kx] * near[None]
             initial = term if initial is None else initial + term
     initial = initial.reshape(UP, UP, deep, cols)
-    constant = primal_step * fidelity * initial * inverse
+    pull = primal_step * inverse
+    constant = pull * fidelity * initial
 
     line = pix * rows - 3 + iota((deep, cols), 0)
-    inside = (line >= 0) & (line < npix * rows)
     inside_last = (line >= 0) & (line < npix * rows - 1)
 
     def tv(step, current):
@@ -428,11 +428,10 @@
             for b in range(UP)
         ]
         grad_y = jnp.concatenate(
-            [jnp.where(inside[None, None], extrap[1:] - extrap[:-1], 0.0), jnp.stack(under)[None]],
-            axis=0,
-        )
-        trial_x = dual_x + dual_step * grad_x
-        trial_y = dual_y + dual_step * grad_y
+            [extrap[1:] - extrap[:-1], jnp.stack(under)[None]], axis=0
+        )
+        trial_x = dual_x + grad_x
+        trial_y = dual_y + grad_y
         square = jnp.maximum(trial_x * trial_x + trial_y * trial_y, 1e-30)
         shrink = jnp.minimum(1.0, tv_bound * lax.rsqrt(square))
         dual_x = trial_x * shrink
@@ -444,11 +443,11 @@
         above = [pltpu.roll(dual_y[UP - 1, b], 1, 0) for b in range(UP)]
         upper = jnp.concatenate([jnp.stack(above)[None], dual_y[:-1]], axis=0)
         divergence = dual_x - left + dual_y - upper
-        updated = (primal + primal_step * divergence) * inverse + constant
-        return (updated, 2.0 * updated - primal, dual_x, dual_y)
+        updated = primal * inverse + divergence * pull + constant
+        return (updated, (2.0 * dual_step) * updated - dual_step * primal, dual_x, dual_y)
 
     zeros = jnp.zeros_like(initial)
-    result = lax.fori_loop(0, TV_ITERS, tv, (initial, initial, zeros, zeros))[0]
+    result = lax.fori_loop(0, TV_ITERS, tv, (initial, dual_step * initial, zeros, zeros))[0]
 
     shape = (fine_rows, UP * deep)
     to, fr = iota(shape, 0), iota(shape, 1)
@@ -518,9 +517,9 @@
             pltpu.SemaphoreType.DMA((2 * REACH + 1, ndisp)),
         ],
         compiler_params=pltpu.CompilerParams(
-            collective_id=0, has_side_effects=True, vmem_limit_bytes=56 * 1024 * 1024
+            collective_id=0, has_side_effects=True, vmem_limit_bytes=40 * 1024 * 1024
         ),
-    )(*args)
+    )(*[pltpu.with_memory_space_constraint(arg, pltpu.HBM) for arg in args])
 
 
 def solution(mesh):

time: 26.1 us -> 24.1 us (0.923)
  local copies, waits for them, and re-layouts: 2.6 us -> 1.19 us
  Pallas kernels: 22.6 us -> 22.1 us
    unnamed x4 -> x2, local copies, waits for them, and re-layouts: 2.6 us -> 1.19 us
    pallas_call x1, Pallas kernels: 22.6 us -> 22.1 us  [local(): pl.pallas_call(functools.partial(kernel, npix, ndisp), out_shape=(jax.Sha...]
where the time goes in v3:
time: 24.1 us; the launch traced here: 23.9 us
  Pallas kernels  22.1 us (92%)
  local copies, waits for them, and re-layouts  1.19 us (5%)
  between operations  0.64 us (3%)
    pallas_call x1, Pallas kernels, local(): pl.pallas_call(functools.partial(kernel, npix, ndisp), out_shape=(jax.Sha...  22.1 us
    unnamed x2, local copies, waits for them, and re-layouts  1.19 us

profile of v3, /device:TPU:0, one launch (start us, length us, event | category | flops | bytes accessed | tf_op | source)
XLA Modules:
  0.0 23.9 jit_solution(9717818144682054478)
XLA Ops:
  0.6 22.1 %shard_map.113 = (f32[2,256]{1,0:T(2,128)S(1)}, f32[8,1024]{1,0:T(8,128)S(1)}) custom-call(s32[8,1024]{1,0:T(8,128)} %left_hbm.1, s32[8,1024]{1,0:T(8,128)} %right_hbm.1, f32[16,16]{1,0:T(8,128)} %featw_hbm.1, bf16[3,3,3,16,16]{4,3,2,1,0:T(8,128)(2,1)} %w1_hbm.1, f32[1,16]{1,0:T(1,128)} %bitcast.3, bf16[3,3,3,16,16]{4,3,2,1,0:T(8,128)(2,1)} %w2_hbm.1, ...), custom_call_target="tpu_custom_call" | custom-call | tf_op jit(solution)/shard_map/pallas_call | solution.py:493
  22.7 0.6 %copy.14 = f32[2,256]{1,0:T(2,128)} copy(f32[2,256]{1,0:T(2,128)S(1)} %get-tuple-element.4) | data formatting | bytes 4096
  23.3 0.6 %copy.15 = f32[8,1024]{1,0:T(8,128)} copy(f32[8,1024]{1,0:T(8,128)S(1)} %get-tuple-element.5) | data formatting | bytes 65536

commit v4 on v3

--- a/solution.py
+++ b/solution.py
@@ -58,7 +58,7 @@
     coarse_ref, out_ref,
     left_ref, right_ref, featw_ref, w1_ref, b1_ref, w2_ref, b2_ref, head_ref, mask_ref, conf_ref,
     load_sem,
-    keep_buf, rows_buf, part_buf, wt_buf, wmat_buf, col_buf, lr_buf, hid_buf, score_buf, mix_buf,
+    keep_buf, rows_buf, part_buf, wt_buf, wmat_buf, col_buf, lr_buf, hid_buf, score_buf, mix_buf, big_buf,
     rows_send, rows_recv, part_send, part_recv,
 ):
     fine_rows, fine_cols = left_ref.shape
@@ -197,6 +197,20 @@
     for n, ref in enumerate((b1_ref, b2_ref, head_ref)):
         col_buf[n] = jnp.broadcast_to(column(ref[...], 4), (group, cols))
 
+    deep = 8
+    taps = mask_ref.shape[1]
+    cc, qq = iota((ch, deep * ch), 0), iota((ch, deep * ch), 1)
+    tiled = dot(mask_ref[...], one_hot(cc == qq % ch), ((0,), (0,)), highest_prec)
+    shape = (taps, deep, deep * ch)
+    big = jnp.where(
+        iota(shape, 1) == iota(shape, 2) // ch, jnp.broadcast_to(tiled[:, None, :], shape), 0.0
+    ).reshape(taps * deep, deep * ch)
+    big_buf[...] = jnp.concatenate(split(big), axis=1)
+
+    step1 = 2 * CHUNK1
+    for n in range(1, step1 + 1):
+        keep_buf[n] = one_hot(iota(keep_buf.shape[1:], 1) >= n).astype(bf16)
+
     def rows_wait(k):
         return pltpu.make_async_remote_copy(
             src_ref=rows_buf.at[1],
@@ -248,17 +262,23 @@
     half = 2 * ch
 
     left_rows = lr_buf[0].astype(bf16)
-    keep_buf[...] = one_hot(iota(keep_buf.shape, 1) >= 1).astype(bf16)
+    def shifted(value, n, inside=None):
+        if n == 0:
+            return value if inside is None else value * inside
+        keep = keep_buf[n] if inside is None else keep_buf[n] * inside
+        rolled = pltpu.roll(value, n, 1)
+        return (rolled.reshape(-1, ch, cols) * keep[None]).reshape(rolled.shape)
 
     def first(c, carry):
-        base = c * (2 * CHUNK1)
-        held, moved = list(carry[:2]), carry[2]
+        base = c * step1
+        held, origin = list(carry[:2]), carry[2]
         for j in range(CHUNK1):
             held = held[-2:]
-            for n in range(2):
-                held.append(moved * left_rows)
-                inside = (start + base + 2 * j + n + 1 < DSP).astype(f32).astype(bf16)
-                moved = pltpu.roll(moved, 1, 1) * (keep_buf[...] * inside)
+            for n in (2 * j, 2 * j + 1):
+                inside = None
+                if n >= step1 - 2:
+                    inside = (start + base + n < DSP).astype(f32).astype(bf16)
+                held.append(shifted(origin, n, inside) * left_rows)
             for rb in range(2):
                 values = jnp.concatenate([v[rb * half : rb * half + vrows] for v in held], axis=0)
                 got = jnp.maximum(conv(wmat_buf[0], values) + col_buf[0], 0.0).astype(bf16)
@@ -266,7 +286,7 @@
                     hid_buf[base + 2 * j + pd, rb * half : (rb + 1) * half, :] = got[
                         pd * half : (pd + 1) * half
                     ]
-        return (held[-2], held[-1], moved)
+        return (held[-2], held[-1], shifted(origin, step1))
 
     opening = jnp.where(
         iota(lr_buf.shape[1:], 1) >= start, pltpu.roll(lr_buf[1], start, 1), 0.0
@@ -350,22 +370,11 @@
             for core in range(ndisp):
                 part_buf[REACH + k, core] = jnp.where(iota((8, cols), 0) < rows, 0.0, 1.0)
 
-    deep = 8
-    taps = mask_ref.shape[1]
-    cc, qq = iota((ch, deep * ch), 0), iota((ch, deep * ch), 1)
-    tiled = dot(mask_ref[...], one_hot(cc == qq % ch), ((0,), (0,)), highest_prec)
-    shape = (taps, deep, deep * ch)
-    big = jnp.where(
-        iota(shape, 1) == iota(shape, 2) // ch, jnp.broadcast_to(tiled[:, None, :], shape), 0.0
-    ).reshape(taps * deep, deep * ch)
     none = jnp.zeros((ch, cols), bf16)
     lines = jnp.concatenate(
         [none] + [rows_buf[slot, 0:frows, :] for slot in range(3)] + [none], axis=0
     )
-    big_high, big_low = split(big)
-    logits = dot(
-        jnp.concatenate([big_high, big_low], axis=1), jnp.concatenate([lines, lines], axis=0)
-    )
+    logits = dot(big_buf[...], jnp.concatenate([lines, lines], axis=0))
     expo = jnp.exp(mask_scale * jnp.tanh(logits)).reshape(9, UP * UP, deep, cols)
     mix_buf[...] = expo * (1.0 / jnp.sum(expo, axis=0))[None]
 
@@ -447,7 +456,9 @@
         return (updated, (2.0 * dual_step) * updated - dual_step * primal, dual_x, dual_y)
 
     zeros = jnp.zeros_like(initial)
-    result = lax.fori_loop(0, TV_ITERS, tv, (initial, dual_step * initial, zeros, zeros))[0]
+    result = lax.fori_loop(
+        0, TV_ITERS, tv, (initial, dual_step * initial, zeros, zeros), unroll=4
+    )[0]
 
     shape = (fine_rows, UP * deep)
     to, fr = iota(shape, 0), iota(shape, 1)
@@ -501,7 +512,7 @@
         scratch_shapes=[pltpu.VMEM(arg.shape, arg.dtype) for arg in args]
         + [
             pltpu.SemaphoreType.DMA((len(args),)),
-            pltpu.VMEM((3 * rows * ch, cols), bf16),
+            pltpu.VMEM((2 * CHUNK1 + 1, ch, cols), bf16),
             pltpu.VMEM((3, 2 * rows * ch + UP * fine_rows, cols), bf16),
             pltpu.VMEM((2 * REACH + 1, ndisp, 8, cols), f32),
             pltpu.VMEM((16 * ch, 16 * ch), f32),
@@ -511,6 +522,7 @@
             pltpu.VMEM((planes + 2, 4 * ch, cols), bf16),
             pltpu.VMEM((planes // 2, 2 * rows, cols), f32),
             pltpu.VMEM((9, UP * UP, 8, cols), f32),
+            pltpu.VMEM((mask_weight.shape[1] * 8, 2 * 8 * ch), bf16),
             pltpu.SemaphoreType.DMA((3,)),
             pltpu.SemaphoreType.DMA((3,)),
             pltpu.SemaphoreType.DMA((2 * REACH + 1, ndisp)),

time: 24.1 us -> 23.5 us (0.975)
  Pallas kernels: 22.1 us -> 21.5 us
    pallas_call x1, Pallas kernels: 22.1 us -> 21.5 us  [local(): pl.pallas_call(functools.partial(kernel, npix, ndisp), out_shape=(jax.Sha...]
where the time goes in v4:
time: 23.5 us; the launch traced here: 23.3 us
  Pallas kernels  21.5 us (91%)
  local copies, waits for them, and re-layouts  1.19 us (5%)
  between operations  0.64 us (3%)
    pallas_call x1, Pallas kernels, local(): pl.pallas_call(functools.partial(kernel, npix, ndisp), out_shape=(jax.Sha...  21.5 us
    unnamed x2, local copies, waits for them, and re-layouts  1.19 us

profile of v4, /device:TPU:0, one launch (start us, length us, event | category | flops | bytes accessed | tf_op | source)
XLA Modules:
  0.0 23.3 jit_solution(6273417051842303508)
XLA Ops:
  0.6 21.5 %shard_map.113 = (f32[2,256]{1,0:T(2,128)S(1)}, f32[8,1024]{1,0:T(8,128)S(1)}) custom-call(s32[8,1024]{1,0:T(8,128)} %left_hbm.1, s32[8,1024]{1,0:T(8,128)} %right_hbm.1, f32[16,16]{1,0:T(8,128)} %featw_hbm.1, bf16[3,3,3,16,16]{4,3,2,1,0:T(8,128)(2,1)} %w1_hbm.1, f32[1,16]{1,0:T(1,128)} %bitcast.3, bf16[3,3,3,16,16]{4,3,2,1,0:T(8,128)(2,1)} %w2_hbm.1, ...), custom_call_target="tpu_custom_call" | custom-call | tf_op jit(solution)/shard_map/pallas_call | solution.py:504
  22.1 0.6 %copy.14 = f32[2,256]{1,0:T(2,128)} copy(f32[2,256]{1,0:T(2,128)S(1)} %get-tuple-element.4) | data formatting | bytes 4096
  22.7 0.6 %copy.15 = f32[8,1024]{1,0:T(8,128)} copy(f32[8,1024]{1,0:T(8,128)S(1)} %get-tuple-element.5) | data formatting | bytes 65536

commit v5 on v4

--- a/solution.py
+++ b/solution.py
@@ -22,7 +22,6 @@
 bf16 = jnp.bfloat16
 LANES = 128
 CHUNK1 = 11
-CHUNK2 = 8
 
 
 def iota(shape, dim):
@@ -58,7 +57,7 @@
     coarse_ref, out_ref,
     left_ref, right_ref, featw_ref, w1_ref, b1_ref, w2_ref, b2_ref, head_ref, mask_ref, conf_ref,
     load_sem,
-    keep_buf, rows_buf, part_buf, wt_buf, wmat_buf, col_buf, lr_buf, hid_buf, score_buf, mix_buf, big_buf,
+    keep_buf, rows_buf, part_buf, wt_buf, wmat_buf, col_buf, bias_buf, lr_buf, score_buf, mix_buf, big_buf,
     rows_send, rows_recv, part_send, part_recv,
 ):
     fine_rows, fine_cols = left_ref.shape
@@ -194,8 +193,23 @@
                             wt_buf[row : row + ch, col : col + ch] = tap
         wmat_buf[n] = wt_buf[...].T[: 12 * ch].astype(bf16)
     group = 4 * ch
-    for n, ref in enumerate((b1_ref, b2_ref, head_ref)):
+    for n, ref in enumerate((b2_ref, head_ref)):
         col_buf[n] = jnp.broadcast_to(column(ref[...], 4), (group, cols))
+    shift1 = jnp.broadcast_to(column(b1_ref[...], 4), (group, cols))
+    place_d = iota((group, cols), 0) // (2 * ch)
+    place_y = iota((group, cols), 0) // ch % 2
+    no_plane = [
+        (place_d == 0) & (disp == 0),
+        (place_d == 1) & (disp == ndisp - 1),
+    ]
+    no_row = [(place_y == 0) & (pix == 0), (place_y == 1) & (pix == npix - 1)]
+    for rb in range(2):
+        for which in range(4):
+            value = jnp.where(no_row[rb], -1e30, shift1)
+            for n in range(2):
+                if which & (n + 1):
+                    value = jnp.where(no_plane[n], -1e30, value)
+            bias_buf[rb, which] = value
 
     deep = 8
     taps = mask_ref.shape[1]
@@ -269,9 +283,11 @@
         rolled = pltpu.roll(value, n, 1)
         return (rolled.reshape(-1, ch, cols) * keep[None]).reshape(rolled.shape)
 
-    def first(c, carry):
+    count = planes // 2 + 1
+
+    def step(c, carry):
         base = c * step1
-        held, origin = list(carry[:2]), carry[2]
+        held, kept, origin = list(carry[:2]), list(carry[2:4]), carry[4]
         for j in range(CHUNK1):
             held = held[-2:]
             for n in (2 * j, 2 * j + 1):
@@ -279,52 +295,37 @@
                 if n >= step1 - 2:
                     inside = (start + base + n < DSP).astype(f32).astype(bf16)
                 held.append(shifted(origin, n, inside) * left_rows)
+            which = 0
+            if j == 0:
+                which = jnp.where(c == 0, 1, 0)
+            if j == CHUNK1 - 1:
+                which = which + jnp.where(c == count // CHUNK1 - 1, 2, 0)
+            parts = []
             for rb in range(2):
                 values = jnp.concatenate([v[rb * half : rb * half + vrows] for v in held], axis=0)
-                got = jnp.maximum(conv(wmat_buf[0], values) + col_buf[0], 0.0).astype(bf16)
-                for pd in range(2):
-                    hid_buf[base + 2 * j + pd, rb * half : (rb + 1) * half, :] = got[
-                        pd * half : (pd + 1) * half
-                    ]
-        return (held[-2], held[-1], shifted(origin, step1))
+                parts.append(
+                    jnp.maximum(conv(wmat_buf[0], values) + bias_buf[rb, which], 0.0).astype(bf16)
+                )
+            kept = kept[-2:] + [
+                jnp.concatenate([v[pd * half : (pd + 1) * half] for v in parts], axis=0)
+                for pd in range(2)
+            ]
+            got = jnp.maximum(conv(wmat_buf[1], jnp.concatenate(kept, axis=0)) + col_buf[0], 0.0)
+            score_buf[c * CHUNK1 + j] = jnp.sum((got * col_buf[1]).reshape(4, ch, cols), axis=1)
+        return (held[-2], held[-1], kept[-2], kept[-1], shifted(origin, step1))
 
     opening = jnp.where(
         iota(lr_buf.shape[1:], 1) >= start, pltpu.roll(lr_buf[1], start, 1), 0.0
     ).astype(bf16)
+    empty = jnp.zeros((vrows, cols), bf16)
     lax.fori_loop(
         0,
-        (planes // 2 + 1) // CHUNK1,
-        first,
-        (volume(start - 2), volume(start - 1), opening),
-    )
-
-    @pl.when(pix == 0)
-    def _():
-        hid_buf[:, 0:ch, :] = jnp.zeros((planes + 2, ch, cols), bf16)
-
-    @pl.when(pix == npix - 1)
-    def _():
-        hid_buf[:, 3 * ch : 4 * ch, :] = jnp.zeros((planes + 2, ch, cols), bf16)
-
-    @pl.when(disp == 0)
-    def _():
-        hid_buf[0] = jnp.zeros((4 * ch, cols), bf16)
-
-    @pl.when(disp == ndisp - 1)
-    def _():
-        hid_buf[planes + 1] = jnp.zeros((4 * ch, cols), bf16)
-
-    def second(c, carry):
-        base = c * CHUNK2
-        for j in range(CHUNK2):
-            values = hid_buf[pl.ds(2 * (base + j), 4)].reshape(4 * vrows, cols)
-            got = jnp.maximum(conv(wmat_buf[1], values) + col_buf[1], 0.0) * col_buf[2]
-            score_buf[base + j] = jnp.sum(got.reshape(4, ch, cols), axis=1)
-        return carry
-
-    lax.fori_loop(0, planes // 2 // CHUNK2, second, 0)
-
-    expo = jnp.exp(-cost_scale * jnp.tanh(score_buf[...]))
+        count // CHUNK1,
+        step,
+        (volume(start - 2), volume(start - 1), empty, empty, opening),
+    )
+
+    expo = jnp.exp(-cost_scale * jnp.tanh(score_buf[1:]))
     shape = expo.shape
     plane = start + 2 * iota(shape, 0) + iota(shape, 1) // rows
     weight4 = jnp.sum(expo, axis=0)
@@ -517,10 +518,10 @@
             pltpu.VMEM((2 * REACH + 1, ndisp, 8, cols), f32),
             pltpu.VMEM((16 * ch, 16 * ch), f32),
             pltpu.VMEM((2, 12 * ch, 16 * ch), bf16),
-            pltpu.VMEM((3, 4 * ch, cols), f32),
+            pltpu.VMEM((2, 4 * ch, cols), f32),
+            pltpu.VMEM((2, 4, 4 * ch, cols), f32),
             pltpu.VMEM((2, 3 * rows * ch, cols), f32),
-            pltpu.VMEM((planes + 2, 4 * ch, cols), bf16),
-            pltpu.VMEM((planes // 2, 2 * rows, cols), f32),
+            pltpu.VMEM((planes // 2 + 1, 2 * rows, cols), f32),
             pltpu.VMEM((9, UP * UP, 8, cols), f32),
             pltpu.VMEM((mask_weight.shape[1] * 8, 2 * 8 * ch), bf16),
             pltpu.SemaphoreType.DMA((3,)),

time: 23.5 us -> 26.2 us (1.11)
  Pallas kernels: 21.5 us -> 24.2 us
    pallas_call x1, Pallas kernels: 21.5 us -> 24.2 us  [local(): pl.pallas_call(functools.partial(kernel, npix, ndisp), out_shape=(jax.Sha...]
where the time goes in v5:
time: 26.2 us; the launch traced here: 26 us
  Pallas kernels  24.2 us (92%)
  local copies, waits for them, and re-layouts  1.19 us (5%)
  between operations  0.64 us (2%)
    pallas_call x1, Pallas kernels, local(): pl.pallas_call(functools.partial(kernel, npix, ndisp), out_shape=(jax.Sha...  24.2 us
    unnamed x2, local copies, waits for them, and re-layouts  1.19 us

profile of v5, /device:TPU:0, one launch (start us, length us, event | category | flops | bytes accessed | tf_op | source)
XLA Modules:
  0.0 26.0 jit_solution(15743074253154039646)
XLA Ops:
  0.6 24.2 %shard_map.113 = (f32[2,256]{1,0:T(2,128)S(1)}, f32[8,1024]{1,0:T(8,128)S(1)}) custom-call(s32[8,1024]{1,0:T(8,128)} %left_hbm.1, s32[8,1024]{1,0:T(8,128)} %right_hbm.1, f32[16,16]{1,0:T(8,128)} %featw_hbm.1, bf16[3,3,3,16,16]{4,3,2,1,0:T(8,128)(2,1)} %w1_hbm.1, f32[1,16]{1,0:T(1,128)} %bitcast.3, bf16[3,3,3,16,16]{4,3,2,1,0:T(8,128)(2,1)} %w2_hbm.1, ...), custom_call_target="tpu_custom_call" | custom-call | tf_op jit(solution)/shard_map/pallas_call | solution.py:505
  24.8 0.6 %copy.14 = f32[2,256]{1,0:T(2,128)} copy(f32[2,256]{1,0:T(2,128)S(1)} %get-tuple-element.4) | data formatting | bytes 4096
  25.4 0.6 %copy.15 = f32[8,1024]{1,0:T(8,128)} copy(f32[8,1024]{1,0:T(8,128)S(1)} %get-tuple-element.5) | data formatting | bytes 65536

commit v6 on v4

--- a/solution.py
+++ b/solution.py
@@ -181,6 +181,8 @@
     for load in loads[4:]:
         load.wait()
 
+    to, fr = iota((12 * ch, 12 * ch), 0), iota((12 * ch, 12 * ch), 1)
+    order = one_hot(fr == (to % 24 // 8) * 4 * ch + to // 24 * 8 + to % 8).astype(bf16)
     for n, w_ref in enumerate((w1_ref, w2_ref)):
         wt_buf[...] = jnp.zeros_like(wt_buf)
         for kd in range(3):
@@ -192,7 +194,8 @@
                             row = ((kd + pd) * 4 + ky + py) * ch
                             col = (kx * 4 + pd * 2 + py) * ch
                             wt_buf[row : row + ch, col : col + ch] = tap
-        wmat_buf[n] = wt_buf[...].T[: 12 * ch].astype(bf16)
+        by_tap = wt_buf[...].T[: 12 * ch].astype(bf16)
+        wmat_buf[n] = dot(order, by_tap).astype(bf16)
     group = 4 * ch
     for n, ref in enumerate((b1_ref, b2_ref, head_ref)):
         col_buf[n] = jnp.broadcast_to(column(ref[...], 4), (group, cols))
@@ -238,18 +241,19 @@
     not_last = lane < LANES - 1
 
     def conv(weights, values):
-        acc = dot(weights, values)
+        acc = dot(weights, values).reshape(group // 8, 3, 8, cols)
+        tap = [acc[:, kx].reshape(group, cols) for kx in range(3)]
         moved_right, moved_left = {}, {}
         parts = []
         for n in range(cols // LANES):
             at = slice(n * LANES, (n + 1) * LANES)
-            moved_right[n] = pltpu.roll(acc[0:group, at], 1, 1)
-            moved_left[n] = pltpu.roll(acc[2 * group :, at], LANES - 1, 1)
+            moved_right[n] = pltpu.roll(tap[0][:, at], 1, 1)
+            moved_left[n] = pltpu.roll(tap[2][:, at], LANES - 1, 1)
         for n in range(cols // LANES):
             at = slice(n * LANES, (n + 1) * LANES)
             before = jnp.where(not_first, moved_right[n], moved_right.get(n - 1, 0.0))
             after = jnp.where(not_last, moved_left[n], moved_left.get(n + 1, 0.0))
-            parts.append(acc[group : 2 * group, at] + before + after)
+            parts.append(tap[1][:, at] + before + after)
         return jnp.concatenate(parts, axis=1)
 
     def volume(plane):

time: 23.5 us -> 23.6 us (level)
  no operation moved by 1% of the time
where the time goes in v6:
time: 23.6 us; the launch traced here: 23.4 us
  Pallas kernels  21.6 us (92%)
  local copies, waits for them, and re-layouts  1.19 us (5%)
  between operations  0.64 us (3%)
    pallas_call x1, Pallas kernels, local(): pl.pallas_call(functools.partial(kernel, npix, ndisp), out_shape=(jax.Sha...  21.6 us
    unnamed x2, local copies, waits for them, and re-layouts  1.19 us

profile of v6, /device:TPU:0, one launch (start us, length us, event | category | flops | bytes accessed | tf_op | source)
XLA Modules:
  0.0 23.4 jit_solution(14536472507628502444)
XLA Ops:
  0.6 21.6 %shard_map.113 = (f32[2,256]{1,0:T(2,128)S(1)}, f32[8,1024]{1,0:T(8,128)S(1)}) custom-call(s32[8,1024]{1,0:T(8,128)} %left_hbm.1, s32[8,1024]{1,0:T(8,128)} %right_hbm.1, f32[16,16]{1,0:T(8,128)} %featw_hbm.1, bf16[3,3,3,16,16]{4,3,2,1,0:T(8,128)(2,1)} %w1_hbm.1, f32[1,16]{1,0:T(1,128)} %bitcast.3, bf16[3,3,3,16,16]{4,3,2,1,0:T(8,128)(2,1)} %w2_hbm.1, ...), custom_call_target="tpu_custom_call" | custom-call | tf_op jit(solution)/shard_map/pallas_call | solution.py:508
  22.2 0.6 %copy.14 = f32[2,256]{1,0:T(2,128)} copy(f32[2,256]{1,0:T(2,128)S(1)} %get-tuple-element.4) | data formatting | bytes 4096
  22.8 0.6 %copy.15 = f32[8,1024]{1,0:T(8,128)} copy(f32[8,1024]{1,0:T(8,128)S(1)} %get-tuple-element.5) | data formatting | bytes 65536

commit v7 on v6

--- a/solution.py
+++ b/solution.py
@@ -240,8 +240,8 @@
     not_first = lane >= 1
     not_last = lane < LANES - 1
 
-    def conv(weights, values):
-        acc = dot(weights, values).reshape(group // 8, 3, 8, cols)
+    def finish(acc):
+        acc = acc.reshape(group // 8, 3, 8, cols)
         tap = [acc[:, kx].reshape(group, cols) for kx in range(3)]
         moved_right, moved_left = {}, {}
         parts = []
@@ -276,6 +276,17 @@
     def first(c, carry):
         base = c * step1
         held, origin = list(carry[:2]), carry[2]
+        waiting = None
+
+        def close(pending):
+            j, accs = pending
+            for rb in range(2):
+                got = jnp.maximum(finish(accs[rb]) + col_buf[0], 0.0).astype(bf16)
+                for pd in range(2):
+                    hid_buf[base + 2 * j + pd, rb * half : (rb + 1) * half, :] = got[
+                        pd * half : (pd + 1) * half
+                    ]
+
         for j in range(CHUNK1):
             held = held[-2:]
             for n in (2 * j, 2 * j + 1):
@@ -283,13 +294,14 @@
                 if n >= step1 - 2:
                     inside = (start + base + n < DSP).astype(f32).astype(bf16)
                 held.append(shifted(origin, n, inside) * left_rows)
+            accs = []
             for rb in range(2):
                 values = jnp.concatenate([v[rb * half : rb * half + vrows] for v in held], axis=0)
-                got = jnp.maximum(conv(wmat_buf[0], values) + col_buf[0], 0.0).astype(bf16)
-                for pd in range(2):
-                    hid_buf[base + 2 * j + pd, rb * half : (rb + 1) * half, :] = got[
-                        pd * half : (pd + 1) * half
-                    ]
+                accs.append(dot(wmat_buf[0], values))
+            if waiting is not None:
+                close(waiting)
+            waiting = (j, accs)
+        close(waiting)
         return (held[-2], held[-1], shifted(origin, step1))
 
     opening = jnp.where(
@@ -320,10 +332,20 @@
 
     def second(c, carry):
         base = c * CHUNK2
+        waiting = None
+
+        def close(pending):
+            j, acc = pending
+            got = jnp.maximum(finish(acc) + col_buf[1], 0.0) * col_buf[2]
+            score_buf[base + j] = jnp.sum(got.reshape(4, ch, cols), axis=1)
+
         for j in range(CHUNK2):
             values = hid_buf[pl.ds(2 * (base + j), 4)].reshape(4 * vrows, cols)
-            got = jnp.maximum(conv(wmat_buf[1], values) + col_buf[1], 0.0) * col_buf[2]
-            score_buf[base + j] = jnp.sum(got.reshape(4, ch, cols), axis=1)
+            acc = dot(wmat_buf[1], values)
+            if waiting is not None:
+                close(waiting)
+            waiting = (j, acc)
+        close(waiting)
         return carry
 
     lax.fori_loop(0, planes // 2 // CHUNK2, second, 0)

time: 23.6 us -> 22.5 us (0.953)
  Pallas kernels: 21.6 us -> 20.5 us
    pallas_call x1, Pallas kernels: 21.6 us -> 20.5 us  [local(): pl.pallas_call(functools.partial(kernel, npix, ndisp), out_shape=(jax.Sha...]
where the time goes in v7:
time: 22.5 us; the launch traced here: 22.4 us
  Pallas kernels  20.5 us (91%)
  local copies, waits for them, and re-layouts  1.19 us (5%)
  between operations  0.64 us (3%)
    pallas_call x1, Pallas kernels, local(): pl.pallas_call(functools.partial(kernel, npix, ndisp), out_shape=(jax.Sha...  20.5 us
    unnamed x2, local copies, waits for them, and re-layouts  1.19 us

profile of v7, /device:TPU:0, one launch (start us, length us, event | category | flops | bytes accessed | tf_op | source)
XLA Modules:
  0.0 22.4 jit_solution(1654955519604126370)
XLA Ops:
  0.6 20.5 %shard_map.113 = (f32[2,256]{1,0:T(2,128)S(1)}, f32[8,1024]{1,0:T(8,128)S(1)}) custom-call(s32[8,1024]{1,0:T(8,128)} %left_hbm.1, s32[8,1024]{1,0:T(8,128)} %right_hbm.1, f32[16,16]{1,0:T(8,128)} %featw_hbm.1, bf16[3,3,3,16,16]{4,3,2,1,0:T(8,128)(2,1)} %w1_hbm.1, f32[1,16]{1,0:T(1,128)} %bitcast.3, bf16[3,3,3,16,16]{4,3,2,1,0:T(8,128)(2,1)} %w2_hbm.1, ...), custom_call_target="tpu_custom_call" | custom-call | tf_op jit(solution)/shard_map/pallas_call | solution.py:530
  21.2 0.6 %copy.14 = f32[2,256]{1,0:T(2,128)} copy(f32[2,256]{1,0:T(2,128)S(1)} %get-tuple-element.4) | data formatting | bytes 4096
  21.7 0.6 %copy.15 = f32[8,1024]{1,0:T(8,128)} copy(f32[8,1024]{1,0:T(8,128)S(1)} %get-tuple-element.5) | data formatting | bytes 65536
